TPU v7x, 256 devices: a whole 4x4x8 slice. The times are simulated.
256 devices in a mesh: member: 16 (over x, y), band: 16 (over z, core).
Axes of the slice: x: 4, y: 4, z: 8, core: 2. Of those that a mesh axis runs over, the one named last changes fastest.
Arguments:
- perturb: bfloat16 [80, 2, 16, 131072], P('member', None, None, 'band'), may hold values from -15 to 15
- control: float32 [2, 16, 131072], P(None, None, 'band'), may hold values from -6 to 6
- static_cov: float32 [2, 16, 16], replicated, may hold values from -1.5 to 1.5
- loc_table: bfloat16 [16, 256, 256], replicated, may hold values from -0.109375 to 0.109375
- pair_offset: int32 [512, 12], P('band'), may hold values from -6 to 6, as said below
- pair_table: int32 [512, 12], P('band'), may hold values from 0 to 15
- pair_count: int32 [512], P('band'), may hold values from 1 to 12, as said below
Outputs:
- increment: float32 [2, 16, 131072], P(None, 'member', 'band')
Inputs may be any that keep to these rules, and one draw needn't show every extreme that they name: `pair_offset`: the offsets of one block are distinct. `pair_count`: counting blocks in aligned runs of 32, the first 6 and the last 6 blocks of every run have all 12 slots live; so do all blocks of some runs, the first run among them.
All inputs are finite; a program needn't handle non-finite values.
Results may differ from a plain program's by a relative error of at most 0.0022.
Values may be sent and summed in bfloat16 or wider, within the bound.
No kernel may reach another device: no remote copies, remote signals or barrier semaphores. Data moves between devices by JAX's collectives and lax.ppermute only.
A program may use at most 128 MiB of HBM per device.

v0:
```python
import jax
import jax.numpy as jnp
from jax import lax
from jax.sharding import PartitionSpec as P

HB = 6


def extended(cells, sides, width):
    for axis, dim in sides:
        count = lax.axis_size(axis)
        head = lax.slice_in_dim(cells, 0, width, axis=dim)
        tail = lax.slice_in_dim(cells, cells.shape[dim] - width, cells.shape[dim], axis=dim)
        cells = jnp.concatenate(
            [
                lax.ppermute(tail, axis, [(i, (i + 1) % count) for i in range(count)]),
                cells,
                lax.ppermute(head, axis, [((i + 1) % count, i) for i in range(count)]),
            ],
            axis=dim,
        )
    return cells


def localize(words, offsets, table_ids, counts, loc_table):
    rows, width = words.shape
    ntables = loc_table.shape[0]
    size = loc_table.shape[1]
    nblk = width // size
    blocks = jnp.transpose(words.reshape(rows, nblk, size), (1, 0, 2))
    padded = extended(blocks, (("band", 0),), HB)
    slot_ids = jnp.arange(offsets.shape[1], dtype=jnp.int32)
    live = slot_ids[None, :] < counts[:, None]
    table_hits = table_ids[:, :, None] == jnp.arange(ntables, dtype=jnp.int32)[None, None, :]

    def one_shift(shift, acc):
        window = lax.dynamic_slice_in_dim(padded, HB + shift, nblk, 0)
        match = (live & (offsets == shift))[:, :, None] & table_hits
        select = jnp.sum(match.astype(jnp.float32), axis=1).astype(jnp.bfloat16)
        tables = jnp.einsum(
            "bt,tij->bij", select, loc_table, preferred_element_type=jnp.float32
        ).astype(jnp.bfloat16)
        prod = jnp.einsum("bri,bij->brj", window, tables, preferred_element_type=jnp.float32)
        return acc + prod

    start_acc = jnp.zeros((nblk, rows, size), jnp.float32)
    result = lax.fori_loop(0, 2 * HB + 1, lambda step, acc: one_shift(step - HB, acc), start_acc)
    return jnp.transpose(result, (1, 0, 2)).reshape(rows, width)


def per_device(perturb, control, static_cov, loc_table, pair_offset, pair_table, pair_count):
    groups = lax.axis_size("member")
    levels = control.shape[1]
    share = levels // groups
    first = lax.axis_index("member") * share
    cov_mine = lax.dynamic_slice_in_dim(static_cov, first, share, 1)
    static = jnp.einsum("fml,flc->fmc", cov_mine, control, precision=lax.Precision.HIGHEST)
    total_members = perturb.shape[0] * groups
    owned = lax.all_to_all(perturb, "member", split_axis=2, concat_axis=0, tiled=True)
    control_mine = lax.dynamic_slice_in_dim(control, first, share, 1)
    words = (owned.astype(jnp.float32) * control_mine[None]).astype(jnp.bfloat16)
    kall, fields, depth, width = words.shape
    spread = localize(
        words.reshape(kall * fields * depth, width), pair_offset, pair_table, pair_count, loc_table
    )
    spread = spread.reshape(kall, fields, depth, width)
    ensemble = jnp.sum(owned.astype(jnp.float32) * spread, axis=0)
    return 0.5 * static + 0.5 * (ensemble / (total_members - 1))


def solution(mesh):
    return jax.shard_map(
        per_device,
        mesh=mesh,
        in_specs=(
            P("member", None, None, "band"),
            P(None, None, "band"),
            P(),
            P(),
            P("band", None),
            P("band", None),
            P("band"),
        ),
        out_specs=P(None, "member", "band"),
        check_vma=False,
    )
```

profile of v0, /device:TPU:97, one launch (start us, length us, event | category | flops | bytes accessed | tf_op | source)
XLA Modules:
  0.0 374.0 jit_solution(4617417134916345321)
XLA Ops:
  0.0 5.4 %copy.41 = bf16[5,2,16,8192]{3,0,1,2:T(8,128)(2,1)} copy(bf16[5,2,16,8192]{3,2,1,0:T(8,128)(2,1)} %param.9) | data formatting | bytes 5242880 | tf_op args[0]
  5.4 6.8 %all-to-all-start = ((bf16[5,2,16,8192]{3,0,1,2:T(8,128)(2,1)}), bf16[5,2,16,8192]{3,0,1,2:T(8,128)(2,1)}, u32[]{:S(2)}, u32[]{:S(2)}) async-start(bf16[5,2,16,8192]{3,0,1,2:T(8,128)(2,1)} %copy.41), calls=%async_computation | async-start | bytes 8388608 | tf_op jit(solution)/shard_map/all_to_all | solution.py:59
  17.2 8.1 %mul.39 = f32[160,32,256]{2,1,0:T(8,128)} reshape(f32[80,2,8192]{2,1,0:T(2,128)} %mul.38) | data formatting | bytes 10485760 | tf_op jit(solution)/shard_map/mul | solution.py:61
  25.3 48.4 %all-to-all-done = bf16[5,2,16,8192]{3,0,1,2:T(8,128)(2,1)} async-done(((bf16[5,2,16,8192]{3,0,1,2:T(8,128)(2,1)}), bf16[5,2,16,8192]{3,0,1,2:T(8,128)(2,1)}, u32[]{:S(2)}, u32[]{:S(2)}) %all-to-all-start) | async-done | bytes 2621472 | tf_op jit(solution)/shard_map/all_to_all | solution.py:59
  73.7 6.2 %convert_bitcast_fusion = f32[16,5,2,1,8192]{4,1,2,0,3:T(8,128)} fusion(bf16[5,2,16,8192]{3,0,1,2:T(8,128)(2,1)} %all-to-all-done), kind=kLoop, calls=%fused_computation.15 | loop fusion | flops 1310720 | bytes 7864320 | tf_op jit(solution)/shard_map/convert_element_type | solution.py:67
  79.9 9.8 %copy.42 = f32[16,5,2,1,8192]{4,2,1,0,3:T(2,128)} copy(f32[16,5,2,1,8192]{4,1,2,0,3:T(8,128)} %convert_bitcast_fusion) | data formatting | bytes 10485760 | tf_op jit(solution)/shard_map/convert_element_type | solution.py:67
  89.7 8.2 %reshape.66 = f32[160,32,256]{2,1,0:T(8,128)} reshape(f32[16,5,2,1,8192]{4,2,1,0,3:T(2,128)} %copy.42) | data formatting | bytes 10485760 | tf_op jit(solution)/shard_map/convert_element_type | solution.py:67
  126.2 222.4 %while.18 = (s32[]{:T(128)}, f32[32,160,256]{2,1,0:T(8,128)}, bf16[44,160,256]{2,0,1:T(8,128)(2,1)}, s32[32,12]{0,1:T(8,128)S(1)}, bf16[16,256,256]{2,0,1:T(8,12...) while((s32[]{:T(128)}, f32[32,160,256]{2,1,0:T(8,128)}, ...), condition=%wide.region_2.0_spmd.clone, body=%wide.region_0.0_spmd.clone.sunk | while | flops 742941312 | bytes 43259932 | solution.py:47
  132.5 9.4 %select_add_fusion.2 = f32[32,160,256]{2,1,0:T(8,128)} fusion(f32[32,160,256]{2,1,0:T(8,128)} %get-tuple-element.364, pred[]{:T(512)S(6)} %compare.3, bf16[32,256,256]{2,0,1:T(8,128)(2,1)} %convolution_convert_fusion.2, bf16[32,160,256]{2,0,1:T(8,128)(2,1)} %constant_dynamic-slice_fusion.3), kind=kOutput, calls=%fused_computation.2.clone.1 | convolution fusion | flops 673710080 | bytes 17301504 | tf_op jit(solution)/shard_map/while/body/eval_jaxpr/bri,bij->brj/dot_general | solution.py:43
  148.2 10.9 %select_add_fusion.2 = f32[32,160,256]{2,1,0:T(8,128)} fusion(f32[32,160,256]{2,1,0:T(8,128)} %get-tuple-element.364, pred[]{:T(512)S(6)} %compare.3, bf16[32,256,256]{2,0,1:T(8,128)(2,1)} %convolution_convert_fusion.2, bf16[32,160,256]{2,0,1:T(8,128)(2,1)} %constant_dynamic-slice_fusion.3), kind=kOutput, calls=%fused_computation.2.clone.1 | convolution fusion | flops 673710080 | bytes 17301504 | tf_op jit(solution)/shard_map/while/body/eval_jaxpr/bri,bij->brj/dot_general | solution.py:43
  165.4 10.9 %select_add_fusion.2 = f32[32,160,256]{2,1,0:T(8,128)} fusion(f32[32,160,256]{2,1,0:T(8,128)} %get-tuple-element.364, pred[]{:T(512)S(6)} %compare.3, bf16[32,256,256]{2,0,1:T(8,128)(2,1)} %convolution_convert_fusion.2, bf16[32,160,256]{2,0,1:T(8,128)(2,1)} %constant_dynamic-slice_fusion.3), kind=kOutput, calls=%fused_computation.2.clone.1 | convolution fusion | flops 673710080 | bytes 17301504 | tf_op jit(solution)/shard_map/while/body/eval_jaxpr/bri,bij->brj/dot_general | solution.py:43
  182.6 10.9 %select_add_fusion.2 = f32[32,160,256]{2,1,0:T(8,128)} fusion(f32[32,160,256]{2,1,0:T(8,128)} %get-tuple-element.364, pred[]{:T(512)S(6)} %compare.3, bf16[32,256,256]{2,0,1:T(8,128)(2,1)} %convolution_convert_fusion.2, bf16[32,160,256]{2,0,1:T(8,128)(2,1)} %constant_dynamic-slice_fusion.3), kind=kOutput, calls=%fused_computation.2.clone.1 | convolution fusion | flops 673710080 | bytes 17301504 | tf_op jit(solution)/shard_map/while/body/eval_jaxpr/bri,bij->brj/dot_general | solution.py:43
  199.9 10.9 %select_add_fusion.2 = f32[32,160,256]{2,1,0:T(8,128)} fusion(f32[32,160,256]{2,1,0:T(8,128)} %get-tuple-element.364, pred[]{:T(512)S(6)} %compare.3, bf16[32,256,256]{2,0,1:T(8,128)(2,1)} %convolution_convert_fusion.2, bf16[32,160,256]{2,0,1:T(8,128)(2,1)} %constant_dynamic-slice_fusion.3), kind=kOutput, calls=%fused_computation.2.clone.1 | convolution fusion | flops 673710080 | bytes 17301504 | tf_op jit(solution)/shard_map/while/body/eval_jaxpr/bri,bij->brj/dot_general | solution.py:43
  217.1 10.9 %select_add_fusion.2 = f32[32,160,256]{2,1,0:T(8,128)} fusion(f32[32,160,256]{2,1,0:T(8,128)} %get-tuple-element.364, pred[]{:T(512)S(6)} %compare.3, bf16[32,256,256]{2,0,1:T(8,128)(2,1)} %convolution_convert_fusion.2, bf16[32,160,256]{2,0,1:T(8,128)(2,1)} %constant_dynamic-slice_fusion.3), kind=kOutput, calls=%fused_computation.2.clone.1 | convolution fusion | flops 673710080 | bytes 17301504 | tf_op jit(solution)/shard_map/while/body/eval_jaxpr/bri,bij->brj/dot_general | solution.py:43
  234.3 10.9 %select_add_fusion.2 = f32[32,160,256]{2,1,0:T(8,128)} fusion(f32[32,160,256]{2,1,0:T(8,128)} %get-tuple-element.364, pred[]{:T(512)S(6)} %compare.3, bf16[32,256,256]{2,0,1:T(8,128)(2,1)} %convolution_convert_fusion.2, bf16[32,160,256]{2,0,1:T(8,128)(2,1)} %constant_dynamic-slice_fusion.3), kind=kOutput, calls=%fused_computation.2.clone.1 | convolution fusion | flops 673710080 | bytes 17301504 | tf_op jit(solution)/shard_map/while/body/eval_jaxpr/bri,bij->brj/dot_general | solution.py:43
  251.5 10.9 %select_add_fusion.2 = f32[32,160,256]{2,1,0:T(8,128)} fusion(f32[32,160,256]{2,1,0:T(8,128)} %get-tuple-element.364, pred[]{:T(512)S(6)} %compare.3, bf16[32,256,256]{2,0,1:T(8,128)(2,1)} %convolution_convert_fusion.2, bf16[32,160,256]{2,0,1:T(8,128)(2,1)} %constant_dynamic-slice_fusion.3), kind=kOutput, calls=%fused_computation.2.clone.1 | convolution fusion | flops 673710080 | bytes 17301504 | tf_op jit(solution)/shard_map/while/body/eval_jaxpr/bri,bij->brj/dot_general | solution.py:43
  268.7 10.9 %select_add_fusion.2 = f32[32,160,256]{2,1,0:T(8,128)} fusion(f32[32,160,256]{2,1,0:T(8,128)} %get-tuple-element.364, pred[]{:T(512)S(6)} %compare.3, bf16[32,256,256]{2,0,1:T(8,128)(2,1)} %convolution_convert_fusion.2, bf16[32,160,256]{2,0,1:T(8,128)(2,1)} %constant_dynamic-slice_fusion.3), kind=kOutput, calls=%fused_computation.2.clone.1 | convolution fusion | flops 673710080 | bytes 17301504 | tf_op jit(solution)/shard_map/while/body/eval_jaxpr/bri,bij->brj/dot_general | solution.py:43
  286.0 10.9 %select_add_fusion.2 = f32[32,160,256]{2,1,0:T(8,128)} fusion(f32[32,160,256]{2,1,0:T(8,128)} %get-tuple-element.364, pred[]{:T(512)S(6)} %compare.3, bf16[32,256,256]{2,0,1:T(8,128)(2,1)} %convolution_convert_fusion.2, bf16[32,160,256]{2,0,1:T(8,128)(2,1)} %constant_dynamic-slice_fusion.3), kind=kOutput, calls=%fused_computation.2.clone.1 | convolution fusion | flops 673710080 | bytes 17301504 | tf_op jit(solution)/shard_map/while/body/eval_jaxpr/bri,bij->brj/dot_general | solution.py:43
  303.2 10.9 %select_add_fusion.2 = f32[32,160,256]{2,1,0:T(8,128)} fusion(f32[32,160,256]{2,1,0:T(8,128)} %get-tuple-element.364, pred[]{:T(512)S(6)} %compare.3, bf16[32,256,256]{2,0,1:T(8,128)(2,1)} %convolution_convert_fusion.2, bf16[32,160,256]{2,0,1:T(8,128)(2,1)} %constant_dynamic-slice_fusion.3), kind=kOutput, calls=%fused_computation.2.clone.1 | convolution fusion | flops 673710080 | bytes 17301504 | tf_op jit(solution)/shard_map/while/body/eval_jaxpr/bri,bij->brj/dot_general | solution.py:43
  320.5 10.9 %select_add_fusion.2 = f32[32,160,256]{2,1,0:T(8,128)} fusion(f32[32,160,256]{2,1,0:T(8,128)} %get-tuple-element.364, pred[]{:T(512)S(6)} %compare.3, bf16[32,256,256]{2,0,1:T(8,128)(2,1)} %convolution_convert_fusion.2, bf16[32,160,256]{2,0,1:T(8,128)(2,1)} %constant_dynamic-slice_fusion.3), kind=kOutput, calls=%fused_computation.2.clone.1 | convolution fusion | flops 673710080 | bytes 17301504 | tf_op jit(solution)/shard_map/while/body/eval_jaxpr/bri,bij->brj/dot_general | solution.py:43
  337.7 10.9 %select_add_fusion.2 = f32[32,160,256]{2,1,0:T(8,128)} fusion(f32[32,160,256]{2,1,0:T(8,128)} %get-tuple-element.364, pred[]{:T(512)S(6)} %compare.3, bf16[32,256,256]{2,0,1:T(8,128)(2,1)} %convolution_convert_fusion.2, bf16[32,160,256]{2,0,1:T(8,128)(2,1)} %constant_dynamic-slice_fusion.3), kind=kOutput, calls=%fused_computation.2.clone.1 | convolution fusion | flops 673710080 | bytes 17301504 | tf_op jit(solution)/shard_map/while/body/eval_jaxpr/bri,bij->brj/dot_general | solution.py:43
  348.6 7.9 %copy.50 = f32[160,32,256]{2,1,0:T(8,128)} copy(f32[160,32,256]{2,0,1:T(8,128)} %bitcast.33) | data formatting | bytes 10485760 | tf_op jit(solution)/shard_map/transpose | solution.py:48
  356.5 7.5 %reshape_reshape.4 = f32[80,2,1,8192]{3,1,0,2:T(2,128)} reshape(f32[160,32,256]{2,1,0:T(8,128)} %copy.50) | data formatting | bytes 10485760 | tf_op jit(solution)/shard_map/reshape;reshape | solution.py:66
  364.0 9.2 %multiply_reduce_fusion = f32[2,8192]{1,0:T(2,128)S(1)} fusion(f32[80,2,1,8192]{3,1,0,2:T(2,128)} %bitcast.34, f32[80,2,1,8192]{3,1,0,2:T(2,128)} %reshape_reshape.4), kind=kLoop, calls=%fused_computation.16 | loop fusion | flops 2605056 | bytes 10551296 | tf_op jit(solution)/shard_map/reduce_sum | solution.py:67
  (111 shorter events, 116.0 us)
Async XLA Ops:
  0.0 12.2 %copy-start = (f32[2,16,8192]{2,1,0:T(8,128)S(1)}, f32[2,16,8192]{2,1,0:T(8,128)}, u32[]{:S(2)}) copy-start(f32[2,16,8192]{2,1,0:T(8,128)} %param.10) | copy-start | bytes 3145732
  5.4 68.3 %all-to-all-start = ((bf16[5,2,16,8192]{3,0,1,2:T(8,128)(2,1)}), bf16[5,2,16,8192]{3,0,1,2:T(8,128)(2,1)}, u32[]{:S(2)}, u32[]{:S(2)}) async-start(bf16[5,2,16,8192]{3,0,1,2:T(8,128)(2,1)} %copy.41), calls=%async_computation | async-start | bytes 8388608 | tf_op jit(solution)/shard_map/all_to_all | solution.py:59
  102.8 1.5 copy-start.3
  105.5 11.2 %collective-permute-start = (bf16[6,160,256]{2,1,0:T(8,128)(2,1)}, bf16[6,160,256]{2,1,0:T(8,128)(2,1)}, u32[]{:S(2)}, u32[]{:S(2)}) collective-permute-start(bf16[6,160,256]{2,1,0:T(8,128)(2,1)} %copy.44), channel_id=1, source_target_pairs={{0,1},{1,2},{2,3},{3,4},{4,5},{5,6},{6,7},{7,8},{8,9},{9,10},{10,1... | collective-permute-start | bytes 1474568 | tf_op jit(solution)/shard_map/ppermute | solution.py:16
  111.5 9.8 %collective-permute-start.1 = (bf16[6,160,256]{2,1,0:T(8,128)(2,1)}, bf16[6,160,256]{2,1,0:T(8,128)(2,1)}, u32[]{:S(2)}, u32[]{:S(2)}) collective-permute-start(bf16[6,160,256]{2,1,0:T(8,128)(2,1)} %copy.45), channel_id=1, source_target_pairs={{1,0},{2,1},{3,2},{4,3},{5,4},{6,5},{7,6},{8,7},{9,8},{10,9},{11,1... | collective-permute-start | bytes 1474568 | tf_op jit(solution)/shard_map/ppermute | solution.py:18
  111.5 11.1 %copy-start.4 = (bf16[32,160,256]{2,0,1:T(8,128)(2,1)S(1)}, bf16[32,160,256]{2,0,1:T(8,128)(2,1)}, u32[]{:S(2)}) copy-start(bf16[32,160,256]{2,0,1:T(8,128)(2,1)} %copy-done.3) | copy-start | bytes 7864324
  122.6 3.6 copy-start.5
  122.6 3.6 copy-start.6
  122.6 3.6 copy-start.7
  126.2 3.3 copy-start.2
  141.9 3.3 copy-start.2
  159.1 3.3 copy-start.2
  176.3 3.3 copy-start.2
  193.6 3.3 copy-start.2
  210.8 3.3 copy-start.2
  228.0 3.3 copy-start.2
  245.2 3.3 copy-start.2
  262.4 3.3 copy-start.2
  279.6 3.3 copy-start.2
  296.9 3.3 copy-start.2
  314.1 3.3 copy-start.2
  331.4 3.3 copy-start.2
  364.0 10.0 %copy-start.1 = (f32[2,16,8192]{2,1,0:T(8,128)S(1)}, f32[2,16,8192]{2,1,0:T(8,128)}, u32[]{:S(2)}) copy-start(f32[2,16,8192]{2,1,0:T(8,128)} %param.10) | copy-start | bytes 3145732
where the time goes:
time: 378 us; the launch traced here: 374 us
  matrix products  183 us (48%)
  local copies, waits for them, and re-layouts  101 us (27%)
  waiting for transfers between devices  52.6 us (14%)
  other arithmetic  24.6 us (7%)
  starting transfers between devices  11.9 us (3%)
    dot_general x13, matrix products, one_shift(): jnp.einsum('bri,bij->brj', window, tables, preferred_element_type=jnp.flo...  140 us
    all_to_all x1, waiting for transfers between devices, per_device(): lax.all_to_all(perturb, 'member', split_axis=2, concat_axis=0, tiled=True)  48.4 us
    dot_general x13, matrix products, one_shift(): jnp.einsum('bt,tij->bij', select, loc_table, preferred_element_type=jnp.f...  41.9 us
    dynamic_slice x13, local copies, waits for them, and re-layouts, one_shift(): window = lax.dynamic_slice_in_dim(padded, HB + shift, nblk, 0)  39.6 us
    convert_element_type x2, local copies, waits for them, and re-layouts, per_device(): ensemble = jnp.sum(owned.astype(jnp.float32) * spread, axis=0)  17.9 us
    mul x2, local copies, waits for them, and re-layouts, per_device(): owned.astype(jnp.float32) * control_mine[None]  12.9 us
    unnamed x17, local copies, waits for them, and re-layouts  9.92 us
    reduce_sum x1, other arithmetic, per_device(): ensemble = jnp.sum(owned.astype(jnp.float32) * spread, axis=0)  9.22 us
  transfers between devices with their start and end apart: 3, of which 3 were waited for; matrix products, arithmetic and copies ran while one was open for 5% of the time, Pallas kernels for 0%

commit v1 on v0

v1 whole, which is shorter than its diff:
```python
import functools

import jax
import jax.numpy as jnp
from jax import lax
from jax.experimental import pallas as pl
from jax.experimental.pallas import tpu as pltpu
from jax.sharding import PartitionSpec as P

HB = 6
COLS = 256
LANES = 128


def fetch(copies):
    for copy in copies:
        copy.start()
    for copy in copies:
        copy.wait()


def block_term(b, nslots, zero_block, offs, tabs, cnts, words, tables, perturb, part, scale):
    count = cnts[b]
    acc = None
    for s in range(nslots):
        c = jnp.where(s < count, HB + b + offs[b, s], zero_block)
        lhs = words[:, pl.ds(pl.multiple_of(c * COLS, COLS), COLS)]
        prod = jnp.dot(lhs, tables[tabs[b, s]], preferred_element_type=jnp.float32)
        acc = prod if acc is None else acc + prod
    cols = pl.ds(pl.multiple_of(b * COLS, COLS), COLS)
    members = perturb.shape[0]
    fl = perturb.shape[1]
    total = None
    for k in range(members):
        term = perturb[k, :, cols].astype(jnp.float32) * acc[k * fl : (k + 1) * fl]
        total = term if total is None else total + term
    total = total * scale
    rows_per_level = part.shape[0] // 16
    per_field = rows_per_level // 2
    for f in range(2):
        for l0 in (0, 8):
            for h in range(COLS // LANES):
                r = f * 16 + l0
                start = l0 * rows_per_level + f * per_field + (COLS // LANES) * b + h
                part[pl.ds(start, 8, stride=rows_per_level), :] = total[
                    r : r + 8, h * LANES : (h + 1) * LANES
                ]


def inner_kernel(
    scale, member, cov, offs_in, tabs_in, cnts_in, perturb, control, tables,
    words, part, static, offs, tabs, cnts, sems,
):
    fetch([
        pltpu.make_async_copy(offs_in, offs, sems.at[0]),
        pltpu.make_async_copy(tabs_in, tabs, sems.at[1]),
        pltpu.make_async_copy(cnts_in, cnts, sems.at[2]),
    ])
    members, fl, width = perturb.shape
    nblk = width // COLS
    zero_block = nblk + 2 * HB
    words[:, zero_block * COLS : (zero_block + 1) * COLS] = jnp.zeros(
        (words.shape[0], COLS), words.dtype
    )
    row = lax.broadcasted_iota(jnp.int32, (fl, LANES), 0)
    me = member[0]
    weights = jnp.zeros((fl, LANES), jnp.float32)
    for f in range(2):
        for l in range(16):
            weights = jnp.where(row == f * 16 + l, 0.5 * cov[f, me * 16 + l], weights)
    per_field = static.shape[0] // 2

    def form(b, carry):
        for h in range(COLS // LANES):
            cols = pl.ds(pl.multiple_of(b * COLS + h * LANES, LANES), LANES)
            dst = pl.ds(pl.multiple_of((HB + b) * COLS + h * LANES, LANES), LANES)
            ctl = control[:, cols]
            for k in range(members):
                words[k * fl : (k + 1) * fl, dst] = (
                    perturb[k, :, cols].astype(jnp.float32) * ctl
                ).astype(jnp.bfloat16)
            own = weights * ctl
            for f in range(2):
                line = jnp.sum(own[f * 16 : (f + 1) * 16], axis=0, keepdims=True)
                static[pl.ds(f * per_field + (COLS // LANES) * b + h, 1), :] = line
        return carry

    lax.fori_loop(0, nblk, form, 0)

    def step(i, carry):
        for u in range(4):
            block_term(
                HB + i * 4 + u, offs.shape[1], zero_block, offs, tabs, cnts,
                words, tables, perturb, part, scale,
            )
        return carry

    lax.fori_loop(0, (nblk - 2 * HB) // 4, step, 0)


def edge_kernel(
    scale, offs_in, tabs_in, cnts_in, left, right, perturb, tables, words_in, part_in,
    out, words, part, offs, tabs, cnts, sems,
):
    del words_in, part_in
    members, fl, width = perturb.shape
    nblk = width // COLS
    zero_block = nblk + 2 * HB
    fetch([
        pltpu.make_async_copy(offs_in, offs, sems.at[0]),
        pltpu.make_async_copy(tabs_in, tabs, sems.at[1]),
        pltpu.make_async_copy(cnts_in, cnts, sems.at[2]),
        pltpu.make_async_copy(left, words.at[:, pl.ds(0, HB * COLS)], sems.at[3]),
        pltpu.make_async_copy(
            right, words.at[:, pl.ds((HB + nblk) * COLS, HB * COLS)], sems.at[4]
        ),
    ])

    def step(i, carry):
        for u in range(HB):
            block_term(
                i * (nblk - HB) + u, offs.shape[1], zero_block, offs, tabs, cnts,
                words, tables, perturb, part, scale,
            )
        return carry

    lax.fori_loop(0, 2, step, 0)
    rows = out.shape[1]

    def pack(m, carry):
        out[m] = part[pl.ds(pl.multiple_of(m * rows, rows), rows), :].astype(out.dtype)
        return carry

    lax.fori_loop(0, out.shape[0], pack, 0)


def per_device(perturb, control, static_cov, loc_table, pair_offset, pair_table, pair_count):
    groups = lax.axis_size("member")
    bands = lax.axis_size("band")
    members, fields, levels, width = perturb.shape
    fl = fields * levels
    nblk = width // COLS
    slots = pair_offset.shape[1]
    lines = fields * width // LANES
    scale = 0.5 / (members * groups - 1)
    perturb = perturb.reshape(members, fl, width)
    control = control.reshape(fl, width)
    edge = HB * COLS

    def form(lo):
        p = lax.slice_in_dim(perturb, lo, lo + edge, axis=2).astype(jnp.float32)
        c = lax.slice_in_dim(control, lo, lo + edge, axis=1)
        return (p * c[None]).astype(jnp.bfloat16).reshape(members * fl, edge)

    up = [(i, (i + 1) % bands) for i in range(bands)]
    down = [((i + 1) % bands, i) for i in range(bands)]
    left = lax.ppermute(form(width - edge), "band", up)
    right = lax.ppermute(form(0), "band", down)

    me = lax.axis_index("member").astype(jnp.int32).reshape(1)
    vmem = pl.BlockSpec(memory_space=pltpu.VMEM)
    smem = pl.BlockSpec(memory_space=pltpu.SMEM)
    anym = pl.BlockSpec(memory_space=pl.ANY)
    tables_scratch = [
        pltpu.SMEM((nblk, slots), jnp.int32),
        pltpu.SMEM((nblk, slots), jnp.int32),
        pltpu.SMEM((nblk,), jnp.int32),
    ]
    words_shape = jax.ShapeDtypeStruct((members * fl, (nblk + 2 * HB + 1) * COLS), jnp.bfloat16)
    part_shape = jax.ShapeDtypeStruct((levels * lines, LANES), jnp.float32)
    words, part, static = pl.pallas_call(
        functools.partial(inner_kernel, scale),
        out_shape=(words_shape, part_shape, jax.ShapeDtypeStruct((lines, LANES), jnp.float32)),
        in_specs=[smem, smem, anym, anym, anym, vmem, vmem, vmem],
        out_specs=(vmem, vmem, vmem),
        scratch_shapes=tables_scratch + [pltpu.SemaphoreType.DMA((3,))],
        compiler_params=pltpu.CompilerParams(vmem_limit_bytes=32 * 2**20),
        cost_estimate=pl.CostEstimate(
            flops=2 * members * fl * COLS * COLS * slots * (nblk - 2 * HB),
            bytes_accessed=12 * 2**20, transcendentals=0,
        ),
    )(
        me, static_cov.reshape(fields, levels * levels), pair_offset, pair_table, pair_count,
        perturb, control, loc_table,
    )
    partial, _, _ = pl.pallas_call(
        functools.partial(edge_kernel, scale),
        out_shape=(
            jax.ShapeDtypeStruct((levels, lines, LANES), jnp.bfloat16), words_shape, part_shape
        ),
        in_specs=[anym] * 5 + [vmem] * 4,
        out_specs=(vmem, vmem, vmem),
        scratch_shapes=tables_scratch + [pltpu.SemaphoreType.DMA((5,))],
        input_output_aliases={7: 1, 8: 2},
        compiler_params=pltpu.CompilerParams(vmem_limit_bytes=32 * 2**20),
        cost_estimate=pl.CostEstimate(
            flops=2 * members * fl * COLS * COLS * slots * 2 * HB,
            bytes_accessed=8 * 2**20, transcendentals=0,
        ),
    )(pair_offset, pair_table, pair_count, left, right, perturb, loc_table, words, part)
    owned = lax.all_to_all(partial, "member", split_axis=0, concat_axis=0, tiled=True)
    total = jnp.sum(owned.astype(jnp.float32), axis=0) + static
    return total.reshape(fields, 1, width)


def solution(mesh):
    return jax.shard_map(
        per_device,
        mesh=mesh,
        in_specs=(
            P("member", None, None, "band"),
            P(None, None, "band"),
            P(),
            P(),
            P("band", None),
            P("band", None),
            P("band"),
        ),
        out_specs=P(None, "member", "band"),
        check_vma=False,
    )
```

time: 378 us -> 43.7 us (0.12)
  matrix products: 183 us -> 0 us
  local copies, waits for them, and re-layouts: 101 us -> 4.28 us
  waiting for transfers between devices: 52.6 us -> 0.01 us
  other arithmetic: 24.6 us -> 3.03 us
  blocking collectives: 0 us -> 17.9 us
  Pallas kernels: 0 us -> 14.7 us
  starting transfers between devices: 11.9 us -> 3.41 us
    dot_general x27 -> x0, matrix products: 183 us -> none  [the longest x13 140 us: one_shift(): jnp.einsum('bri,bij->brj', window, tables, preferred_element_type=jnp.flo...]
    all_to_all x1 -> x0, waiting for transfers between devices: 48.4 us -> none  [per_device(): lax.all_to_all(perturb, 'member', split_axis=2, concat_axis=0, tiled=True)]
    dynamic_slice x14 -> x0, local copies, waits for them, and re-layouts: 39.6 us -> none  [the longest x13 39.6 us: one_shift(): window = lax.dynamic_slice_in_dim(padded, HB + shift, nblk, 0)]
    all_to_all x0 -> x1, blocking collectives: none -> 17.9 us  [per_device(): lax.all_to_all(partial, 'member', split_axis=0, concat_axis=0, tiled=True)]
    convert_element_type x2 -> x0, local copies, waits for them, and re-layouts: 17.9 us -> none  [per_device(): ensemble = jnp.sum(owned.astype(jnp.float32) * spread, axis=0)]
    pallas_call x0 -> x2, Pallas kernels: none -> 14.7 us  [the longest x1 9.62 us: per_device(): pl.pallas_call(functools.partial(inner_kernel, scale), out_shape=(words_s...]
    mul x2 -> x0, local copies, waits for them, and re-layouts: 12.9 us -> none  [per_device(): owned.astype(jnp.float32) * control_mine[None]]
    reduce_sum x14 -> x1, other arithmetic: 9.63 us -> 0.08 us  [per_device(): total = jnp.sum(owned.astype(jnp.float32), axis=0) + static]
  transfers between devices with their start and end apart: 3 -> 2, of which waited for: 3 -> 0; matrix products, arithmetic and copies ran while one was open for 5% -> 1% of each run, Pallas kernels for 0% -> 22%
where the time goes in v1:
time: 43.7 us; the launch traced here: 43.4 us
  blocking collectives  17.9 us (41%)
  Pallas kernels  14.7 us (34%)
  local copies, waits for them, and re-layouts  4.28 us (10%)
  starting transfers between devices  3.41 us (8%)
  other arithmetic  3.03 us (7%)
    all_to_all x1, blocking collectives, per_device(): lax.all_to_all(partial, 'member', split_axis=0, concat_axis=0, tiled=True)  17.9 us
    pallas_call x1, Pallas kernels, per_device(): pl.pallas_call(functools.partial(inner_kernel, scale), out_shape=(words_s...  9.62 us
    pallas_call x1, Pallas kernels, per_device(): pl.pallas_call(functools.partial(edge_kernel, scale), out_shape=(jax.Shap...  5.09 us
    ppermute x1, starting transfers between devices, per_device(): left = lax.ppermute(form(width - edge), 'band', up)  3.41 us
    unnamed x16, local copies, waits for them, and re-layouts  3 us
    convert_element_type x1, other arithmetic, form(): return (p * c[None]).astype(jnp.bfloat16).reshape(members * fl, edge)  2.31 us
    slice x1, local copies, waits for them, and re-layouts, form(): c = lax.slice_in_dim(control, lo, lo + edge, axis=1)  1.2 us
  transfers between devices with their start and end apart: 2, of which 0 were waited for; matrix products, arithmetic and copies ran while one was open for 1% of the time, Pallas kernels for 22%

profile of v1, /device:TPU:97, one launch (start us, length us, event | category | flops | bytes accessed | tf_op | source)
XLA Modules:
  0.0 43.4 jit_solution(17538027276922813611)
XLA Ops:
  0.0 0.0 copy-start
  0.0 0.0 copy-start.6
  0.0 0.0 copy-start.3
  0.0 1.2 %fusion = (f32[32,1536]{1,0:T(8,128)S(1)}, f32[32,1536]{1,0:T(8,128)S(1)}) fusion(f32[32,8192]{1,0:T(8,128)} %bitcast.9), kind=kLoop, calls=%fused_computation.3 | loop fusion | bytes 786432 | tf_op jit(solution)/shard_map/slice | solution.py:152
  1.2 2.3 %multiply_convert_fusion = (bf16[5,32,1536]{2,1,0:T(8,128)(2,1)}, bf16[5,32,1536]{2,1,0:T(8,128)(2,1)}) fusion(bf16[5,32,8192]{2,1,0:T(8,128)(2,1)} %bitcast.6, f32[32,1536]{1,0:T(8,128)S(1)} %get-tuple-element.15, f32[32,1536]{1,0:T(8,128)S(1)} %get-tuple-element.16), kind=kLoop, calls=%fused_computation.1 | loop fusion | flops 1474560 | bytes 2359296 | tf_op jit(solution)/shard_map/convert_element_type | solution.py:153
  3.5 3.4 %collective-permute-start = (bf16[160,1536]{1,0:T(8,128)(2,1)}, bf16[160,1536]{1,0:T(8,128)(2,1)S(1)}, u32[]{:S(2)}, u32[]{:S(2)}) collective-permute-start(bf16[160,1536]{1,0:T(8,128)(2,1)} %bitcast.2), channel_id=1, source_target_pairs={{0,1},{1,2},{2,3},{3,4},{4,5},{5,6},{6,7},{7,8},{8,9},{9,10},{10,1... | collective-permute-start | bytes 1474568 | tf_op jit(solution)/shard_map/ppermute | solution.py:157
  7.0 0.0 collective-permute-start.1
  7.0 0.0 copy-done.4
  7.0 0.1 reshape.28.cov
  7.0 0.0 copy-done.5
  7.0 0.1 copy.12.offs_in
  7.1 0.0 copy-done.6
  7.1 0.1 copy.13.tabs_in
  7.2 0.0 copy-done
  7.2 0.0 copy-done.3
  7.2 1.2 %copy-done.1 = f32[2,16,8192]{2,1,0:T(8,128)S(1)} copy-done((f32[2,16,8192]{2,1,0:T(8,128)S(1)}, f32[2,16,8192]{2,1,0:T(8,128)}, u32[]{:S(2)}) %copy-start.1) | copy-done | bytes 1048600
  8.5 1.6 %copy-done.2 = bf16[16,256,256]{2,1,0:T(8,128)(2,1)S(1)} copy-done((bf16[16,256,256]{2,1,0:T(8,128)(2,1)S(1)}, bf16[16,256,256]{2,1,0:T(8,128)(2,1)}, u32[]{:S(2)}) %copy-start.2) | copy-done | bytes 2097176
  10.0 9.6 %shard_map.73 = (bf16[160,11520]{1,0:T(8,128)(2,1)S(1)}, f32[2048,128]{1,0:T(8,128)S(1)}, f32[128,128]{1,0:T(8,128)S(1)}) custom-call(s32[1]{0:T(128)} %bitcast.4.member, f32[2,256]{1,0:T(2,128)S(1)} %reshape.28.cov, s32[32,12]{1,0:T(8,128)S(1)} %copy.12.offs_in, s32[32,12]{1,0:T(8,128)S(1)} %copy.13.tabs_in, s32[32]{0:T(128)S(1)} %copy-done.3, ...), custom_call_target="tpu_custom_call" | custom-call | flops 5033164800 | bytes 12582912 | tf_op jit(solution)/shard_map/pallas_call | solution.py:171
  19.7 0.0 collective-permute-done.left
  19.7 0.0 collective-permute-done.1.right
  19.7 5.1 %shard_map.74 = (bf16[16,128,128]{2,1,0:T(8,128)(2,1)S(1)}, bf16[160,11520]{1,0:T(8,128)(2,1)S(1)}, f32[2048,128]{1,0:T(8,128)S(1)}) custom-call(s32[32,12]{1,0:T(8,128)S(1)} %copy.12.offs_in, s32[32,12]{1,0:T(8,128)S(1)} %copy.13.tabs_in, s32[32]{0:T(128)S(1)} %copy-done.3, ...), custom_call_target="tpu_custom_call", output_to_operand_aliasing={{1}: (7, {}), {2}: (8, {})} | custom-call | flops 3019898880 | bytes 8388608 | tf_op jit(solution)/shard_map/pallas_call | solution.py:186
  24.8 17.9 %all_to_all.5 = bf16[16,128,128]{2,1,0:T(8,128)(2,1)S(1)} all-to-all(bf16[16,128,128]{2,1,0:T(8,128)(2,1)S(1)} %get-tuple-element.11), channel_id=1, replica_groups=mesh['member'=16,'band'=16] {'member'}, dimensions={0} | all-to-all | bytes 1048576 | tf_op jit(solution)/shard_map/all_to_all | solution.py:201
  42.7 0.1 convert_reduce_fusion
  42.8 0.6 %add.3 = f32[128,128]{1,0:T(8,128)} add(f32[128,128]{1,0:T(8,128)S(1)} %convert_reduce_fusion, f32[128,128]{1,0:T(8,128)S(1)} %get-tuple-element.12) | non-fusion elementwise | flops 16384 | bytes 196608 | tf_op jit(solution)/shard_map/add | solution.py:202
  (4 shorter events, 0.0 us)
Async XLA Ops:
  0.0 7.2 %copy-start = (bf16[5,2,16,8192]{3,2,1,0:T(8,128)(2,1)S(1)}, bf16[5,2,16,8192]{3,2,1,0:T(8,128)(2,1)}, u32[]{:S(2)}) copy-start(bf16[5,2,16,8192]{3,2,1,0:T(8,128)(2,1)} %param.7) | copy-start | bytes 7864324
  0.0 7.0 %copy-start.4 = (f32[2,16,16]{2,1,0:T(8,128)S(1)}, f32[2,16,16]{2,1,0:T(8,128)}, u32[]{:S(2)}) copy-start(f32[2,16,16]{2,1,0:T(8,128)} %param.9) | copy-start | bytes 6148
  0.0 7.0 %copy-start.5 = (s32[32,12]{0,1:T(8,128)S(1)}, s32[32,12]{0,1:T(8,128)}, u32[]{:S(2)}) copy-start(s32[32,12]{0,1:T(8,128)} %param.11) | copy-start | bytes 4612
  0.0 7.1 %copy-start.6 = (s32[32,12]{0,1:T(8,128)S(1)}, s32[32,12]{0,1:T(8,128)}, u32[]{:S(2)}) copy-start(s32[32,12]{0,1:T(8,128)} %param.12) | copy-start | bytes 4612
  0.0 7.2 %copy-start.3 = (s32[32]{0:T(128)S(1)}, s32[32]{0:T(128)}, u32[]{:S(2)}) copy-start(s32[32]{0:T(128)} %cnts_in.3) | copy-start | bytes 388
  3.5 16.1 %collective-permute-start = (bf16[160,1536]{1,0:T(8,128)(2,1)}, bf16[160,1536]{1,0:T(8,128)(2,1)S(1)}, u32[]{:S(2)}, u32[]{:S(2)}) collective-permute-start(bf16[160,1536]{1,0:T(8,128)(2,1)} %bitcast.2), channel_id=1, source_target_pairs={{0,1},{1,2},{2,3},{3,4},{4,5},{5,6},{6,7},{7,8},{8,9},{9,10},{10,1... | collective-permute-start | bytes 1474568 | tf_op jit(solution)/shard_map/ppermute | solution.py:157
  7.0 12.7 %collective-permute-start.1 = (bf16[160,1536]{1,0:T(8,128)(2,1)}, bf16[160,1536]{1,0:T(8,128)(2,1)}, u32[]{:S(2)}, u32[]{:S(2)}) collective-permute-start(bf16[160,1536]{1,0:T(8,128)(2,1)} %bitcast.3), channel_id=1, source_target_pairs={{1,0},{2,1},{3,2},{4,3},{5,4},{6,5},{7,6},{8,7},{9,8},{10,9},{11,1... | collective-permute-start | bytes 1474568 | tf_op jit(solution)/shard_map/ppermute | solution.py:158
  7.2 1.2 %copy-start.1 = (f32[2,16,8192]{2,1,0:T(8,128)S(1)}, f32[2,16,8192]{2,1,0:T(8,128)}, u32[]{:S(2)}) copy-start(f32[2,16,8192]{2,1,0:T(8,128)} %param.8) | copy-start | bytes 3145732
  8.5 1.6 %copy-start.2 = (bf16[16,256,256]{2,1,0:T(8,128)(2,1)S(1)}, bf16[16,256,256]{2,1,0:T(8,128)(2,1)}, u32[]{:S(2)}) copy-start(bf16[16,256,256]{2,1,0:T(8,128)(2,1)} %tables.3) | copy-start | bytes 6291460

commit v2 on v0

v2 whole, which is shorter than its diff:
```python
import functools

import jax
import jax.numpy as jnp
from jax import lax
from jax.experimental import pallas as pl
from jax.experimental.pallas import tpu as pltpu
from jax.sharding import PartitionSpec as P

HB = 6
COLS = 256
LANES = 128
HALVES = COLS // LANES
LOAD_MIB = 16


def form_words(perturb, control, cols):
    members, fl = perturb.shape[0], perturb.shape[1]
    ctl = control[:, cols]
    return [
        (slice(k * fl, (k + 1) * fl), (perturb[k, :, cols].astype(jnp.float32) * ctl).astype(jnp.bfloat16))
        for k in range(members)
    ]


def block_term(b, zero_block, offs, tabs, cnts, words, tables, perturb, part, scale):
    count = cnts[b]
    acc = None
    for s in range(offs.shape[0]):
        c = jnp.where(s < count, HB + b + offs[s, b], zero_block)
        lhs = words[:, pl.ds(pl.multiple_of(c * COLS, COLS), COLS)]
        prod = jnp.dot(lhs, tables[tabs[s, b]], preferred_element_type=jnp.float32)
        acc = prod if acc is None else acc + prod
    cols = pl.ds(pl.multiple_of(b * COLS, COLS), COLS)
    members, fl = perturb.shape[0], perturb.shape[1]
    total = None
    for k in range(members):
        term = perturb[k, :, cols].astype(jnp.float32) * acc[k * fl : (k + 1) * fl]
        total = term if total is None else total + term
    total = total * scale
    lines = part.shape[0] // 16
    for f in range(2):
        for l0 in (0, 8):
            for h in range(HALVES):
                r = f * 16 + l0
                start = l0 * lines + f * (lines // 2) + HALVES * b + h
                part[pl.ds(start, 8, stride=lines), :] = total[
                    r : r + 8, h * LANES : (h + 1) * LANES
                ]


def load_kernel(
    perturb_in, control_in, tables_in, head, tail, words, perturb, control, tables, sems
):
    edge = head.shape[1]
    members, fl, width = perturb.shape
    nblk = width // COLS
    chunk = 4 * COLS
    starts = [(0, edge), (width - edge, edge)]
    starts += [(lo, chunk) for lo in range(edge, width - edge, chunk)]
    pieces = []
    for lo, size in starts:
        at = pl.ds(lo, size)
        pieces.append((perturb_in.at[:, :, at], perturb.at[:, :, at]))
        pieces.append((control_in.at[:, at], control.at[:, at]))
    half = tables.shape[0] // 2
    for i in range(2):
        pieces.append((tables_in.at[pl.ds(i * half, half)], tables.at[pl.ds(i * half, half)]))
    copies = [pltpu.make_async_copy(src, dst, sems.at[i]) for i, (src, dst) in enumerate(pieces)]
    for copy in copies:
        copy.start()
    zero = (nblk + 2 * HB) * COLS
    words[:, zero : zero + COLS] = jnp.zeros((words.shape[0], COLS), words.dtype)
    for i, (lo, size) in enumerate(starts):
        copies[2 * i].wait()
        copies[2 * i + 1].wait()

        def form(j, carry, i=i, lo=lo):
            cols = pl.ds(pl.multiple_of(lo + j * LANES, LANES), LANES)
            dst = pl.ds(pl.multiple_of(edge + lo + j * LANES, LANES), LANES)
            for rows, value in form_words(perturb, control, cols):
                words[rows, dst] = value
                if i < 2:
                    send = (head, tail)[i]
                    send[rows, pl.ds(pl.multiple_of(j * LANES, LANES), LANES)] = value
            return carry

        lax.fori_loop(0, size // LANES, form, 0, unroll=2)
    for copy in copies[2 * len(starts) :]:
        copy.wait()


def inner_kernel(
    scale, offs_in, tabs_in, cnts_in, cov_in, words, perturb, control, tables,
    part, static, offs, tabs, cnts, cov, sems,
):
    copies = [
        pltpu.make_async_copy(src, dst, sems.at[i])
        for i, (src, dst) in enumerate(
            ((offs_in, offs), (tabs_in, tabs), (cnts_in, cnts), (cov_in, cov))
        )
    ]
    for copy in copies:
        copy.start()
    _, fl, width = perturb.shape
    nblk = width // COLS
    for copy in copies:
        copy.wait()

    def step(i, carry):
        for u in range(4):
            block_term(
                HB + i * 4 + u, nblk + 2 * HB, offs, tabs, cnts,
                words, tables, perturb, part, scale,
            )
        return carry

    lax.fori_loop(0, (nblk - 2 * HB) // 4, step, 0)

    row = lax.broadcasted_iota(jnp.int32, (fl, LANES), 0)
    me = lax.axis_index("member")
    weights = jnp.zeros((fl, LANES), jnp.float32)
    for f in range(2):
        for l in range(16):
            weights = jnp.where(row == f * 16 + l, 0.5 * cov[f * 16 + me, l], weights)
    lines = static.shape[0]

    def static_line(b, carry):
        for h in range(HALVES):
            own = weights * control[:, pl.ds(pl.multiple_of(b * COLS + h * LANES, LANES), LANES)]
            for f in range(2):
                line = jnp.sum(own[f * 16 : (f + 1) * 16], axis=0, keepdims=True)
                static[pl.ds(f * (lines // 2) + HALVES * b + h, 1), :] = line
        return carry

    lax.fori_loop(0, nblk, static_line, 0, unroll=4)


def edge_kernel(
    scale, offs_in, tabs_in, cnts_in, left, right, perturb, tables, words_in, part_in,
    out, words, part, offs, tabs, cnts, sems,
):
    del words_in, part_in
    copies = [
        pltpu.make_async_copy(src, dst, sems.at[i])
        for i, (src, dst) in enumerate(((offs_in, offs), (tabs_in, tabs), (cnts_in, cnts)))
    ]
    for copy in copies:
        copy.start()
    width = perturb.shape[2]
    nblk = width // COLS
    edge = HB * COLS
    zero_block = nblk + 2 * HB
    words[:, 0:edge] = left[...]
    words[:, width + edge : width + 2 * edge] = right[...]
    for copy in copies:
        copy.wait()

    def step(i, carry):
        for u in range(HB):
            block_term(
                i * (nblk - HB) + u, zero_block, offs, tabs, cnts,
                words, tables, perturb, part, scale,
            )
        return carry

    lax.fori_loop(0, 2, step, 0)
    rows = out.shape[1]

    def pack(m, carry):
        out[m] = part[pl.ds(pl.multiple_of(m * rows, rows), rows), :].astype(out.dtype)
        return carry

    lax.fori_loop(0, out.shape[0], pack, 0, unroll=2)


VMEM = pl.BlockSpec(memory_space=pltpu.VMEM)
ANY = pl.BlockSpec(memory_space=pl.ANY)


def params(mib):
    return pltpu.CompilerParams(vmem_limit_bytes=mib * 2**20)


def cost(flops, nbytes):
    return pl.CostEstimate(flops=flops, bytes_accessed=nbytes, transcendentals=0)


def like(array):
    return pltpu.VMEM(array.shape, array.dtype)


def load(perturb, control, tables):
    members, fl, width = perturb.shape
    edge = HB * COLS
    send = pltpu.VMEM((members * fl, edge), jnp.bfloat16)
    words = pltpu.VMEM((members * fl, width + 2 * edge + COLS), jnp.bfloat16)
    return pl.pallas_call(
        load_kernel,
        out_shape=(send, send, words, like(perturb), like(control), like(tables)),
        in_specs=[ANY] * 3,
        out_specs=(VMEM,) * 6,
        scratch_shapes=[pltpu.SemaphoreType.DMA((2 * (2 + (width - 2 * edge) // (4 * COLS)) + 2,))],
        compiler_params=params(LOAD_MIB),
        cost_estimate=cost(10**6, 12 * 2**20),
    )(*(pltpu.with_memory_space_constraint(x, pltpu.HBM) for x in (perturb, control, tables)))


def index_scratch(offs, cnts):
    return [
        pltpu.SMEM(offs.shape, jnp.int32),
        pltpu.SMEM(offs.shape, jnp.int32),
        pltpu.SMEM(cnts.shape, jnp.int32),
    ]


def inner_blocks(scale, levels, offs, tabs, cnts, cov, words, perturb, control, tables):
    members, fl, width = perturb.shape
    nblk = width // COLS
    lines = fl // levels * width // LANES
    return pl.pallas_call(
        functools.partial(inner_kernel, scale),
        out_shape=(
            pltpu.VMEM((levels * lines, LANES), jnp.float32),
            pltpu.VMEM((lines, LANES), jnp.float32),
        ),
        in_specs=[ANY] * 4 + [VMEM] * 4,
        out_specs=(VMEM, VMEM),
        scratch_shapes=index_scratch(offs, cnts)
        + [pltpu.SMEM(cov.shape, jnp.float32), pltpu.SemaphoreType.DMA((4,))],
        compiler_params=params(16),
        cost_estimate=cost(2 * members * fl * COLS**2 * offs.shape[0] * (nblk - 2 * HB), 12 * 2**20),
    )(offs, tabs, cnts, cov, words, perturb, control, tables)


def edge_blocks(scale, levels, offs, tabs, cnts, left, right, perturb, tables, words, part):
    members, fl, width = perturb.shape
    lines = fl // levels * width // LANES
    return pl.pallas_call(
        functools.partial(edge_kernel, scale),
        out_shape=(
            pltpu.VMEM((levels, lines, LANES), jnp.bfloat16),
            like(words),
            like(part),
        ),
        in_specs=[ANY] * 3 + [VMEM] * 6,
        out_specs=(VMEM, VMEM, VMEM),
        scratch_shapes=index_scratch(offs, cnts) + [pltpu.SemaphoreType.DMA((3,))],
        input_output_aliases={7: 1, 8: 2},
        compiler_params=params(16),
        cost_estimate=cost(2 * members * fl * COLS**2 * offs.shape[0] * 2 * HB, 8 * 2**20),
    )(offs, tabs, cnts, left, right, perturb, tables, words, part)[0]


def per_device(perturb, control, static_cov, loc_table, pair_offset, pair_table, pair_count):
    groups = lax.axis_size("member")
    bands = lax.axis_size("band")
    members, fields, levels, width = perturb.shape
    scale = 0.5 / (members * groups - 1)
    perturb = perturb.reshape(members, fields * levels, width)
    control = control.reshape(fields * levels, width)
    cov = static_cov.reshape(fields * levels, levels)
    offs, tabs = pair_offset.T, pair_table.T

    head, tail, words, perturb, control, tables = load(perturb, control, loc_table)
    up = [(i, (i + 1) % bands) for i in range(bands)]
    down = [((i + 1) % bands, i) for i in range(bands)]
    left = lax.ppermute(tail, "band", up)
    right = lax.ppermute(head, "band", down)
    part, static = inner_blocks(
        scale, levels, offs, tabs, pair_count, cov, words, perturb, control, tables
    )
    partial = edge_blocks(
        scale, levels, offs, tabs, pair_count, left, right, perturb, tables, words, part
    )
    owned = lax.all_to_all(partial, "member", split_axis=0, concat_axis=0, tiled=True)
    total = jnp.sum(owned.astype(jnp.float32), axis=0) + static
    return total.reshape(fields, 1, width)


def solution(mesh):
    return jax.shard_map(
        per_device,
        mesh=mesh,
        in_specs=(
            P("member", None, None, "band"),
            P(None, None, "band"),
            P(),
            P(),
            P("band", None),
            P("band", None),
            P("band"),
        ),
        out_specs=P(None, "member", "band"),
        check_vma=False,
    )
```

time: 378 us -> 37.9 us (0.10); the launches traced: 374 us -> 37.8 us
  matrix products: 183 us -> 0 us
  local copies, waits for them, and re-layouts: 101 us -> 0.02 us
  waiting for transfers between devices: 52.6 us -> 1.4 us
  other arithmetic: 24.6 us -> 0.71 us
  blocking collectives: 0 us -> 16.6 us
  Pallas kernels: 0 us -> 15.6 us
  starting transfers between devices: 11.9 us -> 3.42 us
    dot_general x27 -> x0, matrix products: 183 us -> none  [the longest x13 140 us: one_shift(): jnp.einsum('bri,bij->brj', window, tables, preferred_element_type=jnp.flo...]
    all_to_all x1 -> x0, waiting for transfers between devices: 48.4 us -> none  [per_device(): lax.all_to_all(perturb, 'member', split_axis=2, concat_axis=0, tiled=True)]
    dynamic_slice x14 -> x0, local copies, waits for them, and re-layouts: 39.6 us -> none  [the longest x13 39.6 us: one_shift(): window = lax.dynamic_slice_in_dim(padded, HB + shift, nblk, 0)]
    convert_element_type x2 -> x0, local copies, waits for them, and re-layouts: 17.9 us -> none  [per_device(): ensemble = jnp.sum(owned.astype(jnp.float32) * spread, axis=0)]
    all_to_all x0 -> x1, blocking collectives: none -> 16.6 us  [per_device(): lax.all_to_all(partial, 'member', split_axis=0, concat_axis=0, tiled=True)]
    pallas_call x0 -> x3, Pallas kernels: none -> 15.6 us  [the longest x1 8.02 us: inner_blocks(): pl.pallas_call(functools.partial(inner_kernel, scale), out_shape=(pltpu.V...]
    mul x2 -> x0, local copies, waits for them, and re-layouts: 12.9 us -> none  [per_device(): owned.astype(jnp.float32) * control_mine[None]]
    unnamed x17 -> x8, local copies, waits for them, and re-layouts: 9.92 us -> 0.02 us
  transfers between devices with their start and end apart: 3 -> 2, of which waited for: 3 -> 1; matrix products, arithmetic and copies ran while one was open for 5% -> 0% of each run, Pallas kernels for 0% -> 21%
where the time goes in v2:
time: 37.9 us; the launch traced here: 37.8 us
  blocking collectives  16.6 us (44%)
  Pallas kernels  15.6 us (41%)
  starting transfers between devices  3.42 us (9%)
  waiting for transfers between devices  1.4 us (4%)
  other arithmetic  0.71 us (2%)
    all_to_all x1, blocking collectives, per_device(): lax.all_to_all(partial, 'member', split_axis=0, concat_axis=0, tiled=True)  16.6 us
    pallas_call x1, Pallas kernels, inner_blocks(): pl.pallas_call(functools.partial(inner_kernel, scale), out_shape=(pltpu.V...  8.02 us
    pallas_call x1, Pallas kernels, edge_blocks(): pl.pallas_call(functools.partial(edge_kernel, scale), out_shape=(pltpu.VM...  4.7 us
    ppermute x1, starting transfers between devices, per_device(): left = lax.ppermute(tail, 'band', up)  3.42 us
    pallas_call x1, Pallas kernels, load(): pl.pallas_call(load_kernel, out_shape=(send, send, words, like(perturb),...  2.88 us
    ppermute x1, waiting for transfers between devices, per_device(): right = lax.ppermute(head, 'band', down)  1.4 us
  transfers between devices with their start and end apart: 2, of which 1 were waited for; matrix products, arithmetic and copies ran while one was open for 0% of the time, Pallas kernels for 21%

profile of v2, /device:TPU:97, one launch (start us, length us, event | category | flops | bytes accessed | tf_op | source)
XLA Modules:
  0.0 37.8 jit_solution(10252876573663476575)
XLA Ops:
  0.0 0.0 copy-start
  0.0 0.0 copy-start.1
  0.0 0.0 copy-start.2
  0.0 0.0 copy-start.3
  0.0 2.9 %shard_map.73 = (bf16[160,1536]{1,0:T(8,128)(2,1)S(1)}, bf16[160,1536]{1,0:T(8,128)(2,1)S(1)}, bf16[160,11520]{1,0:T(8,128)(2,1)S(1)}, bf16[5,32,8192]{2,1,0:T(8...) custom-call(bf16[5,32,8192]{2,1,0:T(8,128)(2,1)} %bitcast.11, f32[32,8192]{1,0:T(8,128)} %bitcast.12, ...), custom_call_target="tpu_custom_call" | custom-call | flops 1000000 | bytes 12582912 | tf_op jit(solution)/shard_map/pallas_call | solution.py:198
  2.9 3.4 %collective-permute-start = (bf16[160,1536]{1,0:T(8,128)(2,1)S(1)}, bf16[160,1536]{1,0:T(8,128)(2,1)S(1)}, u32[]{:S(2)}, u32[]{:S(2)}) collective-permute-start(bf16[160,1536]{1,0:T(8,128)(2,1)S(1)} %get-tuple-element.14), channel_id=1, source_target_pairs={{0,1},{1,2},{2,3},{3,4},{4,5},{5,6},{6,7},{7,8},{8,9},{9,10},{10,1... | collective-permute-start | bytes 1474568 | tf_op jit(solution)/shard_map/ppermute | solution.py:268
  6.3 0.0 collective-permute-start.1
  6.3 0.0 copy-done
  6.3 0.0 copy-done.1
  6.3 0.0 copy-done.2
  6.3 0.0 copy-done.3
  6.4 8.0 %shard_map.74 = (f32[2048,128]{1,0:T(8,128)S(1)}, f32[128,128]{1,0:T(8,128)S(1)}) custom-call(s32[12,32]{1,0:T(8,128)S(1)} %bitcast.7, s32[12,32]{1,0:T(8,128)S(1)} %bitcast.9, s32[32]{0:T(128)S(1)} %copy-done.3, f32[32,16]{1,0:T(8,128)S(1)} %bitcast.6, bf16[160,11520]{1,0:T(8,128)(2,1)S(1)} %get-tuple-element.18.words.words_in, ...), custom_call_target="tpu_custom_call" | custom-call | flops 5033164800 | bytes 12582912 | tf_op jit(solution)/shard_map/pallas_call | solution.py:221
  14.4 0.0 collective-permute-done.left
  14.4 1.4 %collective-permute-done.1.right = bf16[160,1536]{1,0:T(8,128)(2,1)S(1)} collective-permute-done((bf16[160,1536]{1,0:T(8,128)(2,1)S(1)}, bf16[160,1536]{1,0:T(8,128)(2,1)S(1)}, u32[]{:S(2)}, u32[]{:S(2)}) %collective-permute-start.1) | collective-permute-done | bytes 491552 | tf_op jit(solution)/shard_map/ppermute | solution.py:269
  15.8 4.7 %shard_map.75 = (bf16[16,128,128]{2,1,0:T(8,128)(2,1)S(1)}, bf16[160,11520]{1,0:T(8,128)(2,1)S(1)}, f32[2048,128]{1,0:T(8,128)S(1)}) custom-call(s32[12,32]{1,0:T(8,128)S(1)} %bitcast.8, s32[12,32]{1,0:T(8,128)S(1)} %bitcast.10, s32[32]{0:T(128)S(1)} %copy-done.3, ...), custom_call_target="tpu_custom_call", output_to_operand_aliasing={{1}: (7, {}), {2}: (8, {})} | custom-call | flops 3019898880 | bytes 8388608 | tf_op jit(solution)/shard_map/pallas_call | solution.py:239
  20.5 16.6 %all_to_all.5 = bf16[16,128,128]{2,1,0:T(8,128)(2,1)S(1)} all-to-all(bf16[16,128,128]{2,1,0:T(8,128)(2,1)S(1)} %get-tuple-element.21), channel_id=1, replica_groups=mesh['member'=16,'band'=16] {'member'}, dimensions={0} | all-to-all | bytes 1048576 | tf_op jit(solution)/shard_map/all_to_all | solution.py:276
  37.1 0.1 convert_reduce_fusion
  37.2 0.6 %add.3 = f32[128,128]{1,0:T(8,128)} add(f32[128,128]{1,0:T(8,128)S(1)} %convert_reduce_fusion, f32[128,128]{1,0:T(8,128)S(1)} %get-tuple-element.22) | non-fusion elementwise | flops 16384 | bytes 196608 | tf_op jit(solution)/shard_map/add | solution.py:277
Async XLA Ops:
  0.0 6.3 %copy-start = (f32[2,16,16]{2,1,0:T(8,128)S(1)}, f32[2,16,16]{2,1,0:T(8,128)}, u32[]{:S(2)}) copy-start(f32[2,16,16]{2,1,0:T(8,128)} %param.9) | copy-start | bytes 6148
  0.0 6.3 %copy-start.1 = (s32[32,12]{0,1:T(8,128)S(1)}, s32[32,12]{0,1:T(8,128)}, u32[]{:S(2)}) copy-start(s32[32,12]{0,1:T(8,128)} %param.11) | copy-start | bytes 4612
  0.0 6.3 %copy-start.2 = (s32[32,12]{0,1:T(8,128)S(1)}, s32[32,12]{0,1:T(8,128)}, u32[]{:S(2)}) copy-start(s32[32,12]{0,1:T(8,128)} %param.12) | copy-start | bytes 4612
  0.0 6.3 %copy-start.3 = (s32[32]{0:T(128)S(1)}, s32[32]{0:T(128)}, u32[]{:S(2)}) copy-start(s32[32]{0:T(128)} %cnts_in.3) | copy-start | bytes 388
  2.9 11.5 %collective-permute-start = (bf16[160,1536]{1,0:T(8,128)(2,1)S(1)}, bf16[160,1536]{1,0:T(8,128)(2,1)S(1)}, u32[]{:S(2)}, u32[]{:S(2)}) collective-permute-start(bf16[160,1536]{1,0:T(8,128)(2,1)S(1)} %get-tuple-element.14), channel_id=1, source_target_pairs={{0,1},{1,2},{2,3},{3,4},{4,5},{5,6},{6,7},{7,8},{8,9},{9,10},{10,1... | collective-permute-start | bytes 1474568 | tf_op jit(solution)/shard_map/ppermute | solution.py:268
  6.3 9.5 %collective-permute-start.1 = (bf16[160,1536]{1,0:T(8,128)(2,1)S(1)}, bf16[160,1536]{1,0:T(8,128)(2,1)S(1)}, u32[]{:S(2)}, u32[]{:S(2)}) collective-permute-start(bf16[160,1536]{1,0:T(8,128)(2,1)S(1)} %get-tuple-element.15), channel_id=1, source_target_pairs={{1,0},{2,1},{3,2},{4,3},{5,4},{6,5},{7,6},{8,7},{9,8},{10,9},{11,1... | collective-permute-start | bytes 1474568 | tf_op jit(solution)/shard_map/ppermute | solution.py:269

commit v3 on v2

v3 whole, which is shorter than its diff:
```python
import functools

import jax
import jax.numpy as jnp
from jax import lax
from jax.experimental import pallas as pl
from jax.experimental.pallas import tpu as pltpu
from jax.sharding import PartitionSpec as P

HB = 6
COLS = 256
LANES = 128
HALVES = COLS // LANES
INNER_RUN = 10


def form_words(perturb, control, cols):
    members, fl = perturb.shape[0], perturb.shape[1]
    ctl = control[:, cols]
    return [
        (slice(k * fl, (k + 1) * fl), (perturb[k, :, cols].astype(jnp.float32) * ctl).astype(jnp.bfloat16))
        for k in range(members)
    ]


def block_term(b, zero_block, offs, tabs, cnts, words, tables, perturb, part, scale):
    count = cnts[b]
    acc = None
    for s in range(offs.shape[0]):
        c = jnp.where(s < count, HB + b + offs[s, b], zero_block)
        lhs = words[:, pl.ds(pl.multiple_of(c * COLS, COLS), COLS)]
        prod = jnp.dot(lhs, tables[tabs[s, b]], preferred_element_type=jnp.float32)
        acc = prod if acc is None else acc + prod
    cols = pl.ds(pl.multiple_of(b * COLS, COLS), COLS)
    members, fl = perturb.shape[0], perturb.shape[1]
    total = None
    for k in range(members):
        term = perturb[k, :, cols].astype(jnp.float32) * acc[k * fl : (k + 1) * fl]
        total = term if total is None else total + term
    total = total * scale
    for h in range(HALVES):
        part[HALVES * b + h] = total[:, h * LANES : (h + 1) * LANES]


def far_is_left():
    return lax.axis_index("band") % 2 == 0


def start_all(sems, pairs):
    copies = [pltpu.make_async_copy(src, dst, sems.at[i]) for i, (src, dst) in enumerate(pairs)]
    for copy in copies:
        copy.start()
    return copies


def load_kernel(
    perturb_in, control_in, tables_in, offs_in, tabs_in, cnts_in, cov_in,
    far, near, words, perturb, control, tables, offs, tabs, cnts, cov, sems,
):
    edge = HB * COLS
    _, _, width = perturb.shape
    chunk = 4 * COLS
    left = far_is_left()
    far_lo = pl.multiple_of(jnp.where(left, 0, width - edge), LANES)
    near_lo = pl.multiple_of(jnp.where(left, width - edge, 0), LANES)
    starts = [(far_lo, edge), (near_lo, edge)]
    starts += [(lo, chunk) for lo in range(edge, width - edge, chunk)]
    pairs = []
    for lo, size in starts:
        at = pl.ds(lo, size)
        pairs.append((perturb_in.at[:, :, at], perturb.at[:, :, at]))
        pairs.append((control_in.at[:, at], control.at[:, at]))
    half = tables.shape[0] // 2
    for i in range(2):
        pairs.append((tables_in.at[pl.ds(i * half, half)], tables.at[pl.ds(i * half, half)]))
    pairs += [(offs_in, offs), (tabs_in, tabs), (cnts_in, cnts), (cov_in, cov)]
    copies = start_all(sems, pairs)
    zero = width + 2 * edge
    words[:, zero : zero + COLS] = jnp.zeros((words.shape[0], COLS), words.dtype)
    for i, (lo, size) in enumerate(starts):
        copies[2 * i].wait()
        copies[2 * i + 1].wait()

        def form(j, carry, i=i, lo=lo):
            cols = pl.ds(pl.multiple_of(lo + j * LANES, LANES), LANES)
            dst = pl.ds(pl.multiple_of(edge + lo + j * LANES, LANES), LANES)
            for rows, value in form_words(perturb, control, cols):
                words[rows, dst] = value
                if i < 2:
                    send = (far, near)[i]
                    send[rows, pl.ds(pl.multiple_of(j * LANES, LANES), LANES)] = value
            return carry

        lax.fori_loop(0, size // LANES, form, 0, unroll=2)
    for copy in copies[2 * len(starts) :]:
        copy.wait()


def inner_kernel(
    scale, offs, tabs, cnts, cov, words, perturb, control, tables, part, static
):
    _, fl, width = perturb.shape
    nblk = width // COLS
    inner = nblk - 2 * HB
    run = INNER_RUN

    def step(i, carry):
        for u in range(run):
            block_term(
                HB + i * run + u, nblk + 2 * HB, offs, tabs, cnts,
                words, tables, perturb, part, scale,
            )
        return carry

    lax.fori_loop(0, inner // run, step, 0)

    row = lax.broadcasted_iota(jnp.int32, (fl, LANES), 0)
    me = lax.axis_index("member")
    weights = jnp.zeros((fl, LANES), jnp.float32)
    for f in range(2):
        for l in range(16):
            weights = jnp.where(row == f * 16 + l, 0.5 * cov[f * 16 + me, l], weights)
    lines = static.shape[0]

    def static_line(b, carry):
        for h in range(HALVES):
            own = weights * control[:, pl.ds(pl.multiple_of(b * COLS + h * LANES, LANES), LANES)]
            for f in range(2):
                line = jnp.sum(own[f * 16 : (f + 1) * 16], axis=0, keepdims=True)
                static[pl.ds(f * (lines // 2) + HALVES * b + h, 1), :] = line
        return carry

    lax.fori_loop(0, nblk, static_line, 0, unroll=4)


def side_blocks(scale, left, offs, tabs, cnts, halo, perturb, tables, words, part):
    width = perturb.shape[2]
    nblk = width // COLS
    edge = HB * COLS
    words[:, pl.ds(pl.multiple_of(jnp.where(left, 0, width + edge), LANES), edge)] = halo[...]
    first = jnp.where(left, 0, nblk - HB)
    for u in range(HB):
        block_term(
            first + u, nblk + 2 * HB, offs, tabs, cnts, words, tables, perturb, part, scale
        )


def near_kernel(scale, offs, tabs, cnts, halo, perturb, tables, words_in, part_in, words, part):
    del words_in, part_in
    side_blocks(
        scale, jnp.logical_not(far_is_left()), offs, tabs, cnts, halo, perturb, tables, words, part
    )


def far_kernel(scale, offs, tabs, cnts, halo, perturb, tables, words_in, part_in, out, words, part):
    del words_in, part_in
    side_blocks(scale, far_is_left(), offs, tabs, cnts, halo, perturb, tables, words, part)
    lines = out.shape[1]
    groups = lines // 2 // 16

    def pack(i, carry):
        f, g = i // groups, i % groups
        for l0 in (0, 8):
            at = pl.ds(pl.multiple_of(f * 16 + l0, 8), 8)
            block = jnp.swapaxes(part[pl.ds(g * 16, 16), at, :], 0, 1).astype(out.dtype)
            out[l0 : l0 + 8, pl.ds(pl.multiple_of(i * 16, 16), 16), :] = block
        return carry

    lax.fori_loop(0, 2 * groups, pack, 0)


VMEM = pl.BlockSpec(memory_space=pltpu.VMEM)
SMEM = pl.BlockSpec(memory_space=pltpu.SMEM)
ANY = pl.BlockSpec(memory_space=pl.ANY)


def params(mib):
    return pltpu.CompilerParams(vmem_limit_bytes=mib * 2**20)


def cost(flops, nbytes):
    return pl.CostEstimate(flops=flops, bytes_accessed=nbytes, transcendentals=0)


def like(array):
    return pltpu.VMEM(array.shape, array.dtype)


def load(perturb, control, tables, offs, tabs, cnts, cov):
    members, fl, width = perturb.shape
    edge = HB * COLS
    send = pltpu.VMEM((members * fl, edge), jnp.bfloat16)
    words = pltpu.VMEM((members * fl, width + 2 * edge + COLS), jnp.bfloat16)
    scalars = (offs, tabs, cnts, cov)
    copies = 2 * (2 + (width - 2 * edge) // (4 * COLS)) + 2 + len(scalars)
    return pl.pallas_call(
        load_kernel,
        out_shape=(send, send, words, like(perturb), like(control), like(tables))
        + tuple(pltpu.SMEM(x.shape, x.dtype) for x in scalars),
        in_specs=[ANY] * 7,
        out_specs=(VMEM,) * 6 + (SMEM,) * 4,
        scratch_shapes=[pltpu.SemaphoreType.DMA((copies,))],
        compiler_params=params(16),
        cost_estimate=cost(10**6, 12 * 2**20),
    )(*(pltpu.with_memory_space_constraint(x, pltpu.HBM) for x in (perturb, control, tables) + scalars))


def block_cost(perturb, offs, blocks):
    members, fl, _ = perturb.shape
    return cost(2 * members * fl * COLS**2 * offs.shape[0] * blocks, blocks * 2**19)


def inner_blocks(scale, offs, tabs, cnts, cov, words, perturb, control, tables):
    _, fl, width = perturb.shape
    lines = width // LANES
    return pl.pallas_call(
        functools.partial(inner_kernel, scale),
        out_shape=(
            pltpu.VMEM((lines, fl, LANES), jnp.float32),
            pltpu.VMEM((2 * lines, LANES), jnp.float32),
        ),
        in_specs=[SMEM] * 4 + [VMEM] * 4,
        out_specs=(VMEM, VMEM),
        compiler_params=params(16),
        cost_estimate=block_cost(perturb, offs, width // COLS - 2 * HB),
    )(offs, tabs, cnts, cov, words, perturb, control, tables)


def near_blocks(scale, offs, tabs, cnts, halo, perturb, tables, words, part):
    return pl.pallas_call(
        functools.partial(near_kernel, scale),
        out_shape=(like(words), like(part)),
        in_specs=[SMEM] * 3 + [VMEM] * 5,
        out_specs=(VMEM, VMEM),
        input_output_aliases={6: 0, 7: 1},
        compiler_params=params(16),
        cost_estimate=block_cost(perturb, offs, HB),
    )(offs, tabs, cnts, halo, perturb, tables, words, part)


def far_blocks(scale, levels, offs, tabs, cnts, halo, perturb, tables, words, part):
    lines = part.shape[0] * part.shape[1] // levels
    return pl.pallas_call(
        functools.partial(far_kernel, scale),
        out_shape=(pltpu.VMEM((levels, lines, LANES), jnp.bfloat16), like(words), like(part)),
        in_specs=[SMEM] * 3 + [VMEM] * 5,
        out_specs=(VMEM, VMEM, VMEM),
        input_output_aliases={6: 1, 7: 2},
        compiler_params=params(16),
        cost_estimate=block_cost(perturb, offs, HB),
    )(offs, tabs, cnts, halo, perturb, tables, words, part)[0]


def per_device(perturb, control, static_cov, loc_table, pair_offset, pair_table, pair_count):
    groups = lax.axis_size("member")
    bands = lax.axis_size("band")
    members, fields, levels, width = perturb.shape
    scale = 0.5 / (members * groups - 1)
    perturb = perturb.reshape(members, fields * levels, width)
    control = control.reshape(fields * levels, width)
    cov = static_cov.reshape(fields * levels, levels)

    far, near, words, perturb, control, tables, offs, tabs, cnts, cov = load(
        perturb, control, loc_table, pair_offset.T, pair_table.T, pair_count, cov
    )
    across = [(i, (i + (1 if i % 2 else -1)) % bands) for i in range(bands)]
    beside = [(i, i - 1 if i % 2 else i + 1) for i in range(bands)]
    far = lax.ppermute(far, "band", across)
    near = lax.ppermute(near, "band", beside)
    part, static = inner_blocks(scale, offs, tabs, cnts, cov, words, perturb, control, tables)
    words, part = near_blocks(scale, offs, tabs, cnts, near, perturb, tables, words, part)
    partial = far_blocks(scale, levels, offs, tabs, cnts, far, perturb, tables, words, part)
    owned = lax.all_to_all(partial, "member", split_axis=0, concat_axis=0, tiled=True)
    total = jnp.sum(owned.astype(jnp.float32), axis=0) + static
    return total.reshape(fields, 1, width)


def solution(mesh):
    return jax.shard_map(
        per_device,
        mesh=mesh,
        in_specs=(
            P("member", None, None, "band"),
            P(None, None, "band"),
            P(),
            P(),
            P("band", None),
            P("band", None),
            P("band"),
        ),
        out_specs=P(None, "member", "band"),
        check_vma=False,
    )
```

time: 37.9 us -> 35.7 us (0.942)
  the two profiles are of different devices: /device:TPU:97 before, /device:TPU:8 now
where the time goes in v3:
time: 35.7 us; the launch traced here: 35.6 us
  blocking collectives  15.9 us (45%)
  Pallas kernels  12.8 us (36%)
  starting transfers between devices  6.05 us (17%)
  other arithmetic  0.71 us (2%)
    all_to_all x1, blocking collectives, per_device(): lax.all_to_all(partial, 'member', split_axis=0, concat_axis=0, tiled=True)  15.9 us
    pallas_call x1, Pallas kernels, inner_blocks(): pl.pallas_call(functools.partial(inner_kernel, scale), out_shape=(pltpu.V...  6.02 us
    ppermute x1, starting transfers between devices, per_device(): far = lax.ppermute(far, 'band', across)  5.96 us
    pallas_call x1, Pallas kernels, load(): pl.pallas_call(load_kernel, out_shape=(send, send, words, like(perturb),...  2.93 us
    pallas_call x1, Pallas kernels, far_blocks(): pl.pallas_call(functools.partial(far_kernel, scale), out_shape=(pltpu.VME...  2.09 us
    pallas_call x1, Pallas kernels, near_blocks(): pl.pallas_call(functools.partial(near_kernel, scale), out_shape=(like(wor...  1.79 us
  transfers between devices with their start and end apart: 2, of which 0 were waited for; matrix products, arithmetic and copies ran while one was open for 0% of the time, Pallas kernels for 22%

profile of v3, /device:TPU:8, one launch (start us, length us, event | category | flops | bytes accessed | tf_op | source)
XLA Modules:
  0.0 35.6 jit_solution(17479872085330602145)
XLA Ops:
  0.0 2.9 %shard_map.73 = (bf16[160,1536]{1,0:T(8,128)(2,1)S(1)}, bf16[160,1536]{1,0:T(8,128)(2,1)S(1)}, bf16[160,11520]{1,0:T(8,128)(2,1)S(1)}, bf16[5,32,8192]{2,1,0:T(8...) custom-call(bf16[5,32,8192]{2,1,0:T(8,128)(2,1)} %bitcast.6, ...), custom_call_target="tpu_custom_call" | custom-call | flops 1000000 | bytes 12582912 | tf_op jit(solution)/shard_map/pallas_call | solution.py:196
  2.9 0.1 collective-permute-start.1
  3.0 6.0 %collective-permute-start = (bf16[160,1536]{1,0:T(8,128)(2,1)S(1)}, bf16[160,1536]{1,0:T(8,128)(2,1)S(1)}, u32[]{:S(2)}, u32[]{:S(2)}) collective-permute-start(bf16[160,1536]{1,0:T(8,128)(2,1)S(1)} %get-tuple-element.23), channel_id=1, source_target_pairs={{0,15},{1,2},{2,1},{3,4},{4,3},{5,6},{6,5},{7,8},{8,7},{9,10},{10,... | collective-permute-start | bytes 1474568 | tf_op jit(solution)/shard_map/ppermute | solution.py:268
  9.0 6.0 %shard_map.74 = (f32[64,32,128]{2,1,0:T(8,128)S(1)}, f32[128,128]{1,0:T(8,128)S(1)}) custom-call(s32[12,32]{1,0:T(8,128)S(4)} %get-tuple-element.20.offs, s32[12,32]{1,0:T(8,128)S(4)} %get-tuple-element.21.tabs, s32[32]{0:T(128)S(4)} %get-tuple-element.22.cnts, f32[32,16]{1,0:T(8,128)S(4)} %get-tuple-element.28.cov, ...), custom_call_target="tpu_custom_call" | custom-call | flops 5033164800 | bytes 10485760 | tf_op jit(solution)/shard_map/pallas_call | solution.py:216
  15.0 0.0 collective-permute-done.1.halo
  15.0 1.8 %shard_map.75 = (bf16[160,11520]{1,0:T(8,128)(2,1)S(1)}, f32[64,32,128]{2,1,0:T(8,128)S(1)}) custom-call(s32[12,32]{1,0:T(8,128)S(4)} %get-tuple-element.20.offs, s32[12,32]{1,0:T(8,128)S(4)} %get-tuple-element.21.tabs, s32[32]{0:T(128)S(4)} %get-tuple-element.22.cnts, ...), custom_call_target="tpu_custom_call", output_to_operand_aliasing={{0}: (6, {}), {1}: (7, {})} | custom-call | flops 1509949440 | bytes 3145728 | tf_op jit(solution)/shard_map/pallas_call | solution.py:230
  16.8 0.0 collective-permute-done.halo
  16.8 2.1 %shard_map.76 = (bf16[16,128,128]{2,1,0:T(8,128)(2,1)S(1)}, bf16[160,11520]{1,0:T(8,128)(2,1)S(1)}, f32[64,32,128]{2,1,0:T(8,128)S(1)}) custom-call(s32[12,32]{1,0:T(8,128)S(4)} %get-tuple-element.20.offs, s32[12,32]{1,0:T(8,128)S(4)} %get-tuple-element.21.tabs, s32[32]{0:T(128)S(4)} %get-tuple-element.22.cnts, ...), custom_call_target="tpu_custom_call", output_to_operand_aliasing={{1}: (6, {}), {2}: (7, {})} | custom-call | flops 1509949440 | bytes 3145728 | tf_op jit(solution)/shard_map/pallas_call | solution.py:243
  18.9 15.9 %all_to_all.5 = bf16[16,128,128]{2,1,0:T(8,128)(2,1)S(1)} all-to-all(bf16[16,128,128]{2,1,0:T(8,128)(2,1)S(1)} %get-tuple-element.33), channel_id=1, replica_groups=mesh['member'=16,'band'=16] {'member'}, dimensions={0} | all-to-all | bytes 1048576 | tf_op jit(solution)/shard_map/all_to_all | solution.py:273
  34.9 0.1 convert_reduce_fusion
  34.9 0.6 %add.3 = f32[128,128]{1,0:T(8,128)} add(f32[128,128]{1,0:T(8,128)S(1)} %convert_reduce_fusion, f32[128,128]{1,0:T(8,128)S(1)} %get-tuple-element.34) | non-fusion elementwise | flops 16384 | bytes 196608 | tf_op jit(solution)/shard_map/add | solution.py:274
Async XLA Ops:
  2.9 12.1 %collective-permute-start.1 = (bf16[160,1536]{1,0:T(8,128)(2,1)S(1)}, bf16[160,1536]{1,0:T(8,128)(2,1)S(1)}, u32[]{:S(2)}, u32[]{:S(2)}) collective-permute-start(bf16[160,1536]{1,0:T(8,128)(2,1)S(1)} %get-tuple-element.26), channel_id=1, source_target_pairs={{0,1},{1,0},{2,3},{3,2},{4,5},{5,4},{6,7},{7,6},{8,9},{9,8},{10,11... | collective-permute-start | bytes 1474568 | tf_op jit(solution)/shard_map/ppermute | solution.py:269
  3.0 13.8 %collective-permute-start = (bf16[160,1536]{1,0:T(8,128)(2,1)S(1)}, bf16[160,1536]{1,0:T(8,128)(2,1)S(1)}, u32[]{:S(2)}, u32[]{:S(2)}) collective-permute-start(bf16[160,1536]{1,0:T(8,128)(2,1)S(1)} %get-tuple-element.23), channel_id=1, source_target_pairs={{0,15},{1,2},{2,1},{3,4},{4,3},{5,6},{6,5},{7,8},{8,7},{9,10},{10,... | collective-permute-start | bytes 1474568 | tf_op jit(solution)/shard_map/ppermute | solution.py:268

commit v4 on v3

--- a/solution.py
+++ b/solution.py
@@ -12,6 +12,8 @@
 LANES = 128
 HALVES = COLS // LANES
 INNER_RUN = 10
+AHEAD_FLOPS = 2 * 10**10
+INNER_FLOPS = 10**5
 
 
 def form_words(perturb, control, cols):
@@ -53,84 +55,129 @@
     return copies
 
 
-def load_kernel(
-    perturb_in, control_in, tables_in, offs_in, tabs_in, cnts_in, cov_in,
-    far, near, words, perturb, control, tables, offs, tabs, cnts, cov, sems,
-):
-    edge = HB * COLS
-    _, _, width = perturb.shape
-    chunk = 4 * COLS
-    left = far_is_left()
-    far_lo = pl.multiple_of(jnp.where(left, 0, width - edge), LANES)
-    near_lo = pl.multiple_of(jnp.where(left, width - edge, 0), LANES)
-    starts = [(far_lo, edge), (near_lo, edge)]
-    starts += [(lo, chunk) for lo in range(edge, width - edge, chunk)]
-    pairs = []
-    for lo, size in starts:
-        at = pl.ds(lo, size)
-        pairs.append((perturb_in.at[:, :, at], perturb.at[:, :, at]))
-        pairs.append((control_in.at[:, at], control.at[:, at]))
-    half = tables.shape[0] // 2
-    for i in range(2):
-        pairs.append((tables_in.at[pl.ds(i * half, half)], tables.at[pl.ds(i * half, half)]))
-    pairs += [(offs_in, offs), (tabs_in, tabs), (cnts_in, cnts), (cov_in, cov)]
-    copies = start_all(sems, pairs)
-    zero = width + 2 * edge
-    words[:, zero : zero + COLS] = jnp.zeros((words.shape[0], COLS), words.dtype)
-    for i, (lo, size) in enumerate(starts):
-        copies[2 * i].wait()
-        copies[2 * i + 1].wait()
-
-        def form(j, carry, i=i, lo=lo):
-            cols = pl.ds(pl.multiple_of(lo + j * LANES, LANES), LANES)
-            dst = pl.ds(pl.multiple_of(edge + lo + j * LANES, LANES), LANES)
-            for rows, value in form_words(perturb, control, cols):
-                words[rows, dst] = value
-                if i < 2:
-                    send = (far, near)[i]
-                    send[rows, pl.ds(pl.multiple_of(j * LANES, LANES), LANES)] = value
-            return carry
-
-        lax.fori_loop(0, size // LANES, form, 0, unroll=2)
-    for copy in copies[2 * len(starts) :]:
-        copy.wait()
-
-
-def inner_kernel(
-    scale, offs, tabs, cnts, cov, words, perturb, control, tables, part, static
-):
-    _, fl, width = perturb.shape
-    nblk = width // COLS
-    inner = nblk - 2 * HB
-    run = INNER_RUN
-
-    def step(i, carry):
-        for u in range(run):
-            block_term(
-                HB + i * run + u, nblk + 2 * HB, offs, tabs, cnts,
-                words, tables, perturb, part, scale,
-            )
+def form_run(lo, size, member_weights, perturb, control, words, static, send=None):
+    edge = HB * COLS
+    lines = static.shape[0] // 2
+
+    def form(j, carry):
+        cols = pl.ds(pl.multiple_of(lo + j * LANES, LANES), LANES)
+        dst = pl.ds(pl.multiple_of(edge + lo + j * LANES, LANES), LANES)
+        for rows, value in form_words(perturb, control, cols):
+            words[rows, dst] = value
+            if send is not None:
+                send[rows, pl.ds(pl.multiple_of(j * LANES, LANES), LANES)] = value
+        own = member_weights * control[:, cols]
+        for f in range(2):
+            line = jnp.sum(own[f * 16 : (f + 1) * 16], axis=0, keepdims=True)
+            static[pl.ds(f * lines + lo // LANES + j, 1), :] = line
         return carry
 
-    lax.fori_loop(0, inner // run, step, 0)
-
+    lax.fori_loop(0, size // LANES, form, 0, unroll=2)
+
+
+def static_weights(cov, fl):
     row = lax.broadcasted_iota(jnp.int32, (fl, LANES), 0)
     me = lax.axis_index("member")
     weights = jnp.zeros((fl, LANES), jnp.float32)
     for f in range(2):
         for l in range(16):
             weights = jnp.where(row == f * 16 + l, 0.5 * cov[f * 16 + me, l], weights)
-    lines = static.shape[0]
-
-    def static_line(b, carry):
-        for h in range(HALVES):
-            own = weights * control[:, pl.ds(pl.multiple_of(b * COLS + h * LANES, LANES), LANES)]
-            for f in range(2):
-                line = jnp.sum(own[f * 16 : (f + 1) * 16], axis=0, keepdims=True)
-                static[pl.ds(f * (lines // 2) + HALVES * b + h, 1), :] = line
+    return weights
+
+
+def edge_kernel(
+    perturb_in, control_in, offs_in, tabs_in, cnts_in, cov_in,
+    far, near, words, static, perturb, offs, tabs, cnts, cov, control, sems,
+):
+    edge = HB * COLS
+    _, fl, width = perturb.shape
+    left = far_is_left()
+    far_lo = pl.multiple_of(jnp.where(left, 0, width - edge), LANES)
+    near_lo = pl.multiple_of(jnp.where(left, width - edge, 0), LANES)
+    sides = ((far_lo, far), (near_lo, near))
+    pairs = [(cov_in, cov)]
+    for lo, _ in sides:
+        at = pl.ds(lo, edge)
+        pairs.append((perturb_in.at[:, :, at], perturb.at[:, :, at]))
+        pairs.append((control_in.at[:, at], control.at[:, at]))
+    pairs += [(offs_in, offs), (tabs_in, tabs), (cnts_in, cnts)]
+    copies = start_all(sems, pairs)
+    zero = width + 2 * edge
+    words[:, zero : zero + COLS] = jnp.zeros((words.shape[0], COLS), words.dtype)
+    copies[0].wait()
+    weights = static_weights(cov, fl)
+    for i, (lo, send) in enumerate(sides):
+        copies[1 + 2 * i].wait()
+        copies[2 + 2 * i].wait()
+        form_run(lo, edge, weights, perturb, control, words, static, send)
+    for copy in copies[5:]:
+        copy.wait()
+
+
+def loads_ahead():
+    band = lax.axis_index("band")
+    return (band == 0) | (band == 7)
+
+
+def rest_of_band(cov, perturb_in, control_in, tables_in, words, static, perturb, tables, control, sems):
+    edge = HB * COLS
+    _, fl, width = perturb.shape
+    chunk = 4 * COLS
+    starts = range(edge, width - edge, chunk)
+    pairs = []
+    for lo in starts:
+        at = pl.ds(lo, chunk)
+        pairs.append((perturb_in.at[:, :, at], perturb.at[:, :, at]))
+        pairs.append((control_in.at[:, at], control.at[:, at]))
+    half = tables.shape[0] // 2
+    for i in range(2):
+        pairs.append((tables_in.at[pl.ds(i * half, half)], tables.at[pl.ds(i * half, half)]))
+    copies = start_all(sems, pairs)
+    weights = static_weights(cov, fl)
+    for i, lo in enumerate(starts):
+        copies[2 * i].wait()
+        copies[2 * i + 1].wait()
+        form_run(lo, chunk, weights, perturb, control, words, static)
+    for copy in copies[2 * len(starts) :]:
+        copy.wait()
+
+
+def ahead_kernel(
+    cov, perturb_in, control_in, tables_in, words_in, static_in, edges_in, far_in,
+    words, static, perturb, far, tables, control, sems,
+):
+    del words_in, static_in, edges_in, far_in, far
+
+    @pl.when(loads_ahead())
+    def _():
+        rest_of_band(
+            cov, perturb_in, control_in, tables_in, words, static, perturb, tables, control, sems
+        )
+
+
+def inner_kernel(
+    scale, offs, tabs, cnts, cov, perturb_in, control_in, tables_in, words_in, static_in, edges_in,
+    tables_mine, words, static, perturb, tables, part, control, sems,
+):
+    del words_in, static_in, edges_in, tables_mine
+
+    @pl.when(jnp.logical_not(loads_ahead()))
+    def _():
+        rest_of_band(
+            cov, perturb_in, control_in, tables_in, words, static, perturb, tables, control, sems
+        )
+
+    nblk = perturb.shape[2] // COLS
+
+    def step(i, carry):
+        for u in range(INNER_RUN):
+            block_term(
+                HB + i * INNER_RUN + u, nblk + 2 * HB, offs, tabs, cnts,
+                words, tables, perturb, part, scale,
+            )
         return carry
 
-    lax.fori_loop(0, nblk, static_line, 0, unroll=4)
+    lax.fori_loop(0, (nblk - 2 * HB) // INNER_RUN, step, 0)
 
 
 def side_blocks(scale, left, offs, tabs, cnts, halo, perturb, tables, words, part):
@@ -186,23 +233,28 @@
     return pltpu.VMEM(array.shape, array.dtype)
 
 
-def load(perturb, control, tables, offs, tabs, cnts, cov):
+def in_hbm(*arrays):
+    return [pltpu.with_memory_space_constraint(x, pltpu.HBM) for x in arrays]
+
+
+def band_edges(perturb, control, offs, tabs, cnts, cov):
     members, fl, width = perturb.shape
     edge = HB * COLS
     send = pltpu.VMEM((members * fl, edge), jnp.bfloat16)
     words = pltpu.VMEM((members * fl, width + 2 * edge + COLS), jnp.bfloat16)
     scalars = (offs, tabs, cnts, cov)
-    copies = 2 * (2 + (width - 2 * edge) // (4 * COLS)) + 2 + len(scalars)
-    return pl.pallas_call(
-        load_kernel,
-        out_shape=(send, send, words, like(perturb), like(control), like(tables))
+    return pl.pallas_call(
+        edge_kernel,
+        out_shape=(
+            send, send, words, pltpu.VMEM((2 * width // LANES, LANES), jnp.float32), like(perturb),
+        )
         + tuple(pltpu.SMEM(x.shape, x.dtype) for x in scalars),
-        in_specs=[ANY] * 7,
-        out_specs=(VMEM,) * 6 + (SMEM,) * 4,
-        scratch_shapes=[pltpu.SemaphoreType.DMA((copies,))],
-        compiler_params=params(16),
-        cost_estimate=cost(10**6, 12 * 2**20),
-    )(*(pltpu.with_memory_space_constraint(x, pltpu.HBM) for x in (perturb, control, tables) + scalars))
+        in_specs=[ANY] * 6,
+        out_specs=(VMEM,) * 5 + (SMEM,) * 4,
+        scratch_shapes=[like(control), pltpu.SemaphoreType.DMA((4 + len(scalars),))],
+        compiler_params=params(16),
+        cost_estimate=cost(10**6, 3 * 2**20),
+    )(*in_hbm(perturb, control, *scalars))
 
 
 def block_cost(perturb, offs, blocks):
@@ -210,20 +262,39 @@
     return cost(2 * members * fl * COLS**2 * offs.shape[0] * blocks, blocks * 2**19)
 
 
-def inner_blocks(scale, offs, tabs, cnts, cov, words, perturb, control, tables):
+def rest_scratch(control):
+    copies = 2 * ((control.shape[1] - 2 * HB * COLS) // (4 * COLS)) + 2
+    return [like(control), pltpu.SemaphoreType.DMA((copies,))]
+
+
+def load_ahead(cov, perturb, control, tables, words, static, edges, far):
+    return pl.pallas_call(
+        ahead_kernel,
+        out_shape=(like(words), like(static), like(perturb), like(far), like(tables)),
+        in_specs=[SMEM] + [ANY] * 3 + [VMEM] * 4,
+        out_specs=(VMEM,) * 5,
+        input_output_aliases={4: 0, 5: 1, 6: 2, 7: 3},
+        scratch_shapes=rest_scratch(control),
+        compiler_params=params(16),
+        cost_estimate=cost(AHEAD_FLOPS, 10**4),
+    )(cov, *in_hbm(perturb, control, tables), words, static, edges, far)
+
+
+def inner_blocks(scale, offs, tabs, cnts, cov, perturb, control, tables, words, static, edges, mine):
     _, fl, width = perturb.shape
-    lines = width // LANES
     return pl.pallas_call(
         functools.partial(inner_kernel, scale),
         out_shape=(
-            pltpu.VMEM((lines, fl, LANES), jnp.float32),
-            pltpu.VMEM((2 * lines, LANES), jnp.float32),
+            like(words), like(static), like(perturb), like(tables),
+            pltpu.VMEM((width // LANES, fl, LANES), jnp.float32),
         ),
-        in_specs=[SMEM] * 4 + [VMEM] * 4,
-        out_specs=(VMEM, VMEM),
-        compiler_params=params(16),
-        cost_estimate=block_cost(perturb, offs, width // COLS - 2 * HB),
-    )(offs, tabs, cnts, cov, words, perturb, control, tables)
+        in_specs=[SMEM] * 4 + [ANY] * 3 + [VMEM] * 4,
+        out_specs=(VMEM,) * 5,
+        input_output_aliases={7: 0, 8: 1, 9: 2, 10: 3},
+        scratch_shapes=rest_scratch(control),
+        compiler_params=params(16),
+        cost_estimate=cost(INNER_FLOPS, 10**4),
+    )(offs, tabs, cnts, cov, *in_hbm(perturb, control, tables), words, static, edges, mine)
 
 
 def near_blocks(scale, offs, tabs, cnts, halo, perturb, tables, words, part):
@@ -260,14 +331,18 @@
     control = control.reshape(fields * levels, width)
     cov = static_cov.reshape(fields * levels, levels)
 
-    far, near, words, perturb, control, tables, offs, tabs, cnts, cov = load(
-        perturb, control, loc_table, pair_offset.T, pair_table.T, pair_count, cov
+    far, near, words, static, edges, offs, tabs, cnts, cov = band_edges(
+        perturb, control, pair_offset.T, pair_table.T, pair_count, cov
     )
     across = [(i, (i + (1 if i % 2 else -1)) % bands) for i in range(bands)]
     beside = [(i, i - 1 if i % 2 else i + 1) for i in range(bands)]
+    near = lax.ppermute(near, "band", beside)
+    whole = (perturb, control, loc_table)
+    words, static, edges, far, tables = load_ahead(cov, *whole, words, static, edges, far)
     far = lax.ppermute(far, "band", across)
-    near = lax.ppermute(near, "band", beside)
-    part, static = inner_blocks(scale, offs, tabs, cnts, cov, words, perturb, control, tables)
+    words, static, perturb, tables, part = inner_blocks(
+        scale, offs, tabs, cnts, cov, *whole, words, static, edges, tables
+    )
     words, part = near_blocks(scale, offs, tabs, cnts, near, perturb, tables, words, part)
     partial = far_blocks(scale, levels, offs, tabs, cnts, far, perturb, tables, words, part)
     owned = lax.all_to_all(partial, "member", split_axis=0, concat_axis=0, tiled=True)

time: 35.7 us -> 34.8 us (0.975)
  the two profiles are of different devices: /device:TPU:8 before, /device:TPU:97 now
where the time goes in v4:
time: 34.8 us; the launch traced here: 34.6 us
  blocking collectives  17.4 us (50%)
  Pallas kernels  13.7 us (39%)
  waiting for transfers between devices  1.43 us (4%)
  starting transfers between devices  1.34 us (4%)
  other arithmetic  0.71 us (2%)
    all_to_all x1, blocking collectives, per_device(): lax.all_to_all(partial, 'member', split_axis=0, concat_axis=0, tiled=True)  17.4 us
    pallas_call x1, Pallas kernels, inner_blocks(): pl.pallas_call(functools.partial(inner_kernel, scale), out_shape=(like(wo...  5.72 us
    pallas_call x1, Pallas kernels, load_ahead(): pl.pallas_call(ahead_kernel, out_shape=(like(words), like(static), like(p...  2.38 us
    pallas_call x1, Pallas kernels, far_blocks(): pl.pallas_call(functools.partial(far_kernel, scale), out_shape=(pltpu.VME...  2.09 us
    pallas_call x1, Pallas kernels, near_blocks(): pl.pallas_call(functools.partial(near_kernel, scale), out_shape=(like(wor...  1.79 us
    pallas_call x1, Pallas kernels, band_edges(): pl.pallas_call(edge_kernel, out_shape=(send, send, words, pltpu.VMEM((2 *...  1.73 us
    ppermute x1, waiting for transfers between devices, per_device(): far = lax.ppermute(far, 'band', across)  1.43 us
    ppermute x1, starting transfers between devices, per_device(): near = lax.ppermute(near, 'band', beside)  0.76 us
  transfers between devices with their start and end apart: 2, of which 1 were waited for; matrix products, arithmetic and copies ran while one was open for 0% of the time, Pallas kernels for 29%

profile of v4, /device:TPU:97, one launch (start us, length us, event | category | flops | bytes accessed | tf_op | source)
XLA Modules:
  0.0 34.6 jit_solution(6643778486273733531)
XLA Ops:
  0.0 1.7 %shard_map.73 = (bf16[160,1536]{1,0:T(8,128)(2,1)S(1)}, bf16[160,1536]{1,0:T(8,128)(2,1)S(1)}, bf16[160,11520]{1,0:T(8,128)(2,1)S(1)}, f32[128,128]{1,0:T(8,128)...) custom-call(bf16[5,32,8192]{2,1,0:T(8,128)(2,1)} %bitcast.6, ...), custom_call_target="tpu_custom_call" | custom-call | flops 1000000 | bytes 3145728 | tf_op jit(solution)/shard_map/pallas_call | solution.py:246
  1.7 0.8 %collective-permute-start.1 = (bf16[160,1536]{1,0:T(8,128)(2,1)S(1)}, bf16[160,1536]{1,0:T(8,128)(2,1)S(1)}, u32[]{:S(2)}, u32[]{:S(2)}) collective-permute-start(bf16[160,1536]{1,0:T(8,128)(2,1)S(1)} %get-tuple-element.42), channel_id=1, source_target_pairs={{0,1},{1,0},{2,3},{3,2},{4,5},{5,4},{6,7},{7,6},{8,9},{9,8},{10,11... | collective-permute-start | bytes 1474568 | tf_op jit(solution)/shard_map/ppermute | solution.py:339
  2.5 2.4 %shard_map.74 = (bf16[160,11520]{1,0:T(8,128)(2,1)S(1)}, f32[128,128]{1,0:T(8,128)S(1)}, bf16[5,32,8192]{2,1,0:T(8,128)(2,1)S(1)}, bf16[160,1536]{1,0:T(8,128)(2,1)S(1)}, bf16[16,256,256]{2,1,0:T(8,128)(2,1)S(1)}) custom-call(f32[32,16]{1,0:T(8,128)S(4)} %get-tuple-element.30.cov, ...), custom_call_target="tpu_custom_call", output_to_operand_aliasing={{0}: (4, {}), {1}: (5, {}), {2}: (6, {}), {3}: (7, {})} | custom-call | flops 20000000000 | bytes 10000 | tf_op jit(solution)/shard_map/pallas_call | solution.py:271
  4.9 0.6 %collective-permute-start = (bf16[160,1536]{1,0:T(8,128)(2,1)S(1)}, bf16[160,1536]{1,0:T(8,128)(2,1)S(1)}, u32[]{:S(2)}, u32[]{:S(2)}) collective-permute-start(bf16[160,1536]{1,0:T(8,128)(2,1)S(1)} %get-tuple-element.35), channel_id=1, source_target_pairs={{0,15},{1,2},{2,1},{3,4},{4,3},{5,6},{6,5},{7,8},{8,7},{9,10},{10,... | collective-permute-start | bytes 1474568 | tf_op jit(solution)/shard_map/ppermute | solution.py:342
  5.5 5.7 %shard_map.75 = (bf16[160,11520]{1,0:T(8,128)(2,1)S(1)}, f32[128,128]{1,0:T(8,128)S(1)}, bf16[5,32,8192]{2,1,0:T(8,128)(2,1)S(1)}, bf16[16,256,256]{2,1,0:T(8,128)(2,1)S(1)}, f32[64,32,128]{2,1,0:T(8,128)S(1)}) custom-call(s32[12,32]{1,0:T(8,128)S(4)} %get-tuple-element.27.offs, ...), custom_call_target="tpu_custom_call", output_to_operand_aliasing={{0}: (7, {}), {1}: (8, {}), {2}: (9, {}), {3}: (10, {})} | custom-call | flops 100000 | bytes 10000 | tf_op jit(solution)/shard_map/pallas_call | solution.py:285
  11.2 0.0 collective-permute-done.1.halo
  11.2 1.8 %shard_map.76 = (bf16[160,11520]{1,0:T(8,128)(2,1)S(1)}, f32[64,32,128]{2,1,0:T(8,128)S(1)}) custom-call(s32[12,32]{1,0:T(8,128)S(4)} %get-tuple-element.27.offs, s32[12,32]{1,0:T(8,128)S(4)} %get-tuple-element.28.tabs, s32[32]{0:T(128)S(4)} %get-tuple-element.29.cnts, ...), custom_call_target="tpu_custom_call", output_to_operand_aliasing={{0}: (6, {}), {1}: (7, {})} | custom-call | flops 1509949440 | bytes 3145728 | tf_op jit(solution)/shard_map/pallas_call | solution.py:301
  13.0 1.4 %collective-permute-done.halo = bf16[160,1536]{1,0:T(8,128)(2,1)S(1)} collective-permute-done((bf16[160,1536]{1,0:T(8,128)(2,1)S(1)}, bf16[160,1536]{1,0:T(8,128)(2,1)S(1)}, u32[]{:S(2)}, u32[]{:S(2)}) %collective-permute-start) | collective-permute-done | bytes 491552 | tf_op jit(solution)/shard_map/ppermute | solution.py:342
  14.4 2.1 %shard_map.77 = (bf16[16,128,128]{2,1,0:T(8,128)(2,1)S(1)}, bf16[160,11520]{1,0:T(8,128)(2,1)S(1)}, f32[64,32,128]{2,1,0:T(8,128)S(1)}) custom-call(s32[12,32]{1,0:T(8,128)S(4)} %get-tuple-element.27.offs, s32[12,32]{1,0:T(8,128)S(4)} %get-tuple-element.28.tabs, s32[32]{0:T(128)S(4)} %get-tuple-element.29.cnts, ...), custom_call_target="tpu_custom_call", output_to_operand_aliasing={{1}: (6, {}), {2}: (7, {})} | custom-call | flops 1509949440 | bytes 3145728 | tf_op jit(solution)/shard_map/pallas_call | solution.py:314
  16.5 17.4 %all_to_all.5 = bf16[16,128,128]{2,1,0:T(8,128)(2,1)S(1)} all-to-all(bf16[16,128,128]{2,1,0:T(8,128)(2,1)S(1)} %get-tuple-element.47), channel_id=1, replica_groups=mesh['member'=16,'band'=16] {'member'}, dimensions={0} | all-to-all | bytes 1048576 | tf_op jit(solution)/shard_map/all_to_all | solution.py:348
  33.9 0.1 convert_reduce_fusion
  34.0 0.6 %add.3 = f32[128,128]{1,0:T(8,128)} add(f32[128,128]{1,0:T(8,128)S(1)} %convert_reduce_fusion, f32[128,128]{1,0:T(8,128)S(1)} %get-tuple-element.48) | non-fusion elementwise | flops 16384 | bytes 196608 | tf_op jit(solution)/shard_map/add | solution.py:349
Async XLA Ops:
  1.7 9.5 %collective-permute-start.1 = (bf16[160,1536]{1,0:T(8,128)(2,1)S(1)}, bf16[160,1536]{1,0:T(8,128)(2,1)S(1)}, u32[]{:S(2)}, u32[]{:S(2)}) collective-permute-start(bf16[160,1536]{1,0:T(8,128)(2,1)S(1)} %get-tuple-element.42), channel_id=1, source_target_pairs={{0,1},{1,0},{2,3},{3,2},{4,5},{5,4},{6,7},{7,6},{8,9},{9,8},{10,11... | collective-permute-start | bytes 1474568 | tf_op jit(solution)/shard_map/ppermute | solution.py:339
  4.9 9.6 %collective-permute-start = (bf16[160,1536]{1,0:T(8,128)(2,1)S(1)}, bf16[160,1536]{1,0:T(8,128)(2,1)S(1)}, u32[]{:S(2)}, u32[]{:S(2)}) collective-permute-start(bf16[160,1536]{1,0:T(8,128)(2,1)S(1)} %get-tuple-element.35), channel_id=1, source_target_pairs={{0,15},{1,2},{2,1},{3,4},{4,3},{5,6},{6,5},{7,8},{8,7},{9,10},{10,... | collective-permute-start | bytes 1474568 | tf_op jit(solution)/shard_map/ppermute | solution.py:342

commit v5 on v4

--- a/solution.py
+++ b/solution.py
@@ -11,7 +11,7 @@
 COLS = 256
 LANES = 128
 HALVES = COLS // LANES
-INNER_RUN = 10
+INNER_RUN = 20
 AHEAD_FLOPS = 2 * 10**10
 INNER_FLOPS = 10**5
 

time: 34.8 us -> 34.7 us (level)
  no operation moved by 1% of the time
where the time goes in v5:
time: 34.7 us; the launch traced here: 34.5 us
  blocking collectives  17.3 us (50%)
  Pallas kernels  13.7 us (39%)
  waiting for transfers between devices  1.49 us (4%)
  starting transfers between devices  1.34 us (4%)
  other arithmetic  0.71 us (2%)
    all_to_all x1, blocking collectives, per_device(): lax.all_to_all(partial, 'member', split_axis=0, concat_axis=0, tiled=True)  17.3 us
    pallas_call x1, Pallas kernels, inner_blocks(): pl.pallas_call(functools.partial(inner_kernel, scale), out_shape=(like(wo...  5.66 us
    pallas_call x1, Pallas kernels, load_ahead(): pl.pallas_call(ahead_kernel, out_shape=(like(words), like(static), like(p...  2.38 us
    pallas_call x1, Pallas kernels, far_blocks(): pl.pallas_call(functools.partial(far_kernel, scale), out_shape=(pltpu.VME...  2.09 us
    pallas_call x1, Pallas kernels, near_blocks(): pl.pallas_call(functools.partial(near_kernel, scale), out_shape=(like(wor...  1.79 us
    pallas_call x1, Pallas kernels, band_edges(): pl.pallas_call(edge_kernel, out_shape=(send, send, words, pltpu.VMEM((2 *...  1.73 us
    ppermute x1, waiting for transfers between devices, per_device(): far = lax.ppermute(far, 'band', across)  1.49 us
    ppermute x1, starting transfers between devices, per_device(): near = lax.ppermute(near, 'band', beside)  0.76 us
  transfers between devices with their start and end apart: 2, of which 1 were waited for; matrix products, arithmetic and copies ran while one was open for 0% of the time, Pallas kernels for 29%

profile of v5, /device:TPU:97, one launch (start us, length us, event | category | flops | bytes accessed | tf_op | source)
XLA Modules:
  0.0 34.5 jit_solution(72635964604494909)
XLA Ops:
  0.0 1.7 %shard_map.73 = (bf16[160,1536]{1,0:T(8,128)(2,1)S(1)}, bf16[160,1536]{1,0:T(8,128)(2,1)S(1)}, bf16[160,11520]{1,0:T(8,128)(2,1)S(1)}, f32[128,128]{1,0:T(8,128)...) custom-call(bf16[5,32,8192]{2,1,0:T(8,128)(2,1)} %bitcast.6, ...), custom_call_target="tpu_custom_call" | custom-call | flops 1000000 | bytes 3145728 | tf_op jit(solution)/shard_map/pallas_call | solution.py:246
  1.7 0.8 %collective-permute-start.1 = (bf16[160,1536]{1,0:T(8,128)(2,1)S(1)}, bf16[160,1536]{1,0:T(8,128)(2,1)S(1)}, u32[]{:S(2)}, u32[]{:S(2)}) collective-permute-start(bf16[160,1536]{1,0:T(8,128)(2,1)S(1)} %get-tuple-element.42), channel_id=1, source_target_pairs={{0,1},{1,0},{2,3},{3,2},{4,5},{5,4},{6,7},{7,6},{8,9},{9,8},{10,11... | collective-permute-start | bytes 1474568 | tf_op jit(solution)/shard_map/ppermute | solution.py:339
  2.5 2.4 %shard_map.74 = (bf16[160,11520]{1,0:T(8,128)(2,1)S(1)}, f32[128,128]{1,0:T(8,128)S(1)}, bf16[5,32,8192]{2,1,0:T(8,128)(2,1)S(1)}, bf16[160,1536]{1,0:T(8,128)(2,1)S(1)}, bf16[16,256,256]{2,1,0:T(8,128)(2,1)S(1)}) custom-call(f32[32,16]{1,0:T(8,128)S(4)} %get-tuple-element.30.cov, ...), custom_call_target="tpu_custom_call", output_to_operand_aliasing={{0}: (4, {}), {1}: (5, {}), {2}: (6, {}), {3}: (7, {})} | custom-call | flops 20000000000 | bytes 10000 | tf_op jit(solution)/shard_map/pallas_call | solution.py:271
  4.9 0.6 %collective-permute-start = (bf16[160,1536]{1,0:T(8,128)(2,1)S(1)}, bf16[160,1536]{1,0:T(8,128)(2,1)S(1)}, u32[]{:S(2)}, u32[]{:S(2)}) collective-permute-start(bf16[160,1536]{1,0:T(8,128)(2,1)S(1)} %get-tuple-element.35), channel_id=1, source_target_pairs={{0,15},{1,2},{2,1},{3,4},{4,3},{5,6},{6,5},{7,8},{8,7},{9,10},{10,... | collective-permute-start | bytes 1474568 | tf_op jit(solution)/shard_map/ppermute | solution.py:342
  5.5 5.7 %shard_map.75 = (bf16[160,11520]{1,0:T(8,128)(2,1)S(1)}, f32[128,128]{1,0:T(8,128)S(1)}, bf16[5,32,8192]{2,1,0:T(8,128)(2,1)S(1)}, bf16[16,256,256]{2,1,0:T(8,128)(2,1)S(1)}, f32[64,32,128]{2,1,0:T(8,128)S(1)}) custom-call(s32[12,32]{1,0:T(8,128)S(4)} %get-tuple-element.27.offs, ...), custom_call_target="tpu_custom_call", output_to_operand_aliasing={{0}: (7, {}), {1}: (8, {}), {2}: (9, {}), {3}: (10, {})} | custom-call | flops 100000 | bytes 10000 | tf_op jit(solution)/shard_map/pallas_call | solution.py:285
  11.1 0.0 collective-permute-done.1.halo
  11.2 1.8 %shard_map.76 = (bf16[160,11520]{1,0:T(8,128)(2,1)S(1)}, f32[64,32,128]{2,1,0:T(8,128)S(1)}) custom-call(s32[12,32]{1,0:T(8,128)S(4)} %get-tuple-element.27.offs, s32[12,32]{1,0:T(8,128)S(4)} %get-tuple-element.28.tabs, s32[32]{0:T(128)S(4)} %get-tuple-element.29.cnts, ...), custom_call_target="tpu_custom_call", output_to_operand_aliasing={{0}: (6, {}), {1}: (7, {})} | custom-call | flops 1509949440 | bytes 3145728 | tf_op jit(solution)/shard_map/pallas_call | solution.py:301
  13.0 1.5 %collective-permute-done.halo = bf16[160,1536]{1,0:T(8,128)(2,1)S(1)} collective-permute-done((bf16[160,1536]{1,0:T(8,128)(2,1)S(1)}, bf16[160,1536]{1,0:T(8,128)(2,1)S(1)}, u32[]{:S(2)}, u32[]{:S(2)}) %collective-permute-start) | collective-permute-done | bytes 491552 | tf_op jit(solution)/shard_map/ppermute | solution.py:342
  14.4 2.1 %shard_map.77 = (bf16[16,128,128]{2,1,0:T(8,128)(2,1)S(1)}, bf16[160,11520]{1,0:T(8,128)(2,1)S(1)}, f32[64,32,128]{2,1,0:T(8,128)S(1)}) custom-call(s32[12,32]{1,0:T(8,128)S(4)} %get-tuple-element.27.offs, s32[12,32]{1,0:T(8,128)S(4)} %get-tuple-element.28.tabs, s32[32]{0:T(128)S(4)} %get-tuple-element.29.cnts, ...), custom_call_target="tpu_custom_call", output_to_operand_aliasing={{1}: (6, {}), {2}: (7, {})} | custom-call | flops 1509949440 | bytes 3145728 | tf_op jit(solution)/shard_map/pallas_call | solution.py:314
  16.5 17.3 %all_to_all.5 = bf16[16,128,128]{2,1,0:T(8,128)(2,1)S(1)} all-to-all(bf16[16,128,128]{2,1,0:T(8,128)(2,1)S(1)} %get-tuple-element.47), channel_id=1, replica_groups=mesh['member'=16,'band'=16] {'member'}, dimensions={0} | all-to-all | bytes 1048576 | tf_op jit(solution)/shard_map/all_to_all | solution.py:348
  33.8 0.1 convert_reduce_fusion
  33.9 0.6 %add.3 = f32[128,128]{1,0:T(8,128)} add(f32[128,128]{1,0:T(8,128)S(1)} %convert_reduce_fusion, f32[128,128]{1,0:T(8,128)S(1)} %get-tuple-element.48) | non-fusion elementwise | flops 16384 | bytes 196608 | tf_op jit(solution)/shard_map/add | solution.py:349
Async XLA Ops:
  1.7 9.4 %collective-permute-start.1 = (bf16[160,1536]{1,0:T(8,128)(2,1)S(1)}, bf16[160,1536]{1,0:T(8,128)(2,1)S(1)}, u32[]{:S(2)}, u32[]{:S(2)}) collective-permute-start(bf16[160,1536]{1,0:T(8,128)(2,1)S(1)} %get-tuple-element.42), channel_id=1, source_target_pairs={{0,1},{1,0},{2,3},{3,2},{4,5},{5,4},{6,7},{7,6},{8,9},{9,8},{10,11... | collective-permute-start | bytes 1474568 | tf_op jit(solution)/shard_map/ppermute | solution.py:339
  4.9 9.6 %collective-permute-start = (bf16[160,1536]{1,0:T(8,128)(2,1)S(1)}, bf16[160,1536]{1,0:T(8,128)(2,1)S(1)}, u32[]{:S(2)}, u32[]{:S(2)}) collective-permute-start(bf16[160,1536]{1,0:T(8,128)(2,1)S(1)} %get-tuple-element.35), channel_id=1, source_target_pairs={{0,15},{1,2},{2,1},{3,4},{4,3},{5,6},{6,5},{7,8},{8,7},{9,10},{10,... | collective-permute-start | bytes 1474568 | tf_op jit(solution)/shard_map/ppermute | solution.py:342

commit v6 on v5

--- a/solution.py
+++ b/solution.py
@@ -192,28 +192,34 @@
         )
 
 
-def near_kernel(scale, offs, tabs, cnts, halo, perturb, tables, words_in, part_in, words, part):
+def pack(group, part, out):
+    groups = out.shape[1] // 2 // 16
+    for f in range(2):
+        for l0 in (0, 8):
+            block = part[pl.ds(pl.multiple_of(group * 16, 16), 16), f * 16 + l0 : f * 16 + l0 + 8, :]
+            rows = pl.ds(pl.multiple_of((f * groups + group) * 16, 16), 16)
+            out[l0 : l0 + 8, rows, :] = jnp.swapaxes(block, 0, 1).astype(out.dtype)
+
+
+def near_kernel(
+    scale, offs, tabs, cnts, halo, perturb, tables, words_in, part_in, words, part, out
+):
     del words_in, part_in
-    side_blocks(
-        scale, jnp.logical_not(far_is_left()), offs, tabs, cnts, halo, perturb, tables, words, part
-    )
-
-
-def far_kernel(scale, offs, tabs, cnts, halo, perturb, tables, words_in, part_in, out, words, part):
-    del words_in, part_in
-    side_blocks(scale, far_is_left(), offs, tabs, cnts, halo, perturb, tables, words, part)
-    lines = out.shape[1]
-    groups = lines // 2 // 16
-
-    def pack(i, carry):
-        f, g = i // groups, i % groups
-        for l0 in (0, 8):
-            at = pl.ds(pl.multiple_of(f * 16 + l0, 8), 8)
-            block = jnp.swapaxes(part[pl.ds(g * 16, 16), at, :], 0, 1).astype(out.dtype)
-            out[l0 : l0 + 8, pl.ds(pl.multiple_of(i * 16, 16), 16), :] = block
-        return carry
-
-    lax.fori_loop(0, 2 * groups, pack, 0)
+    groups = out.shape[1] // 2 // 16
+    for g in range(1, groups - 1):
+        pack(g, part, out)
+    left = jnp.logical_not(far_is_left())
+    side_blocks(scale, left, offs, tabs, cnts, halo, perturb, tables, words, part)
+    pack(jnp.where(left, 0, groups - 1), part, out)
+
+
+def far_kernel(
+    scale, offs, tabs, cnts, halo, perturb, tables, words_in, part_in, out_in, out, words, part
+):
+    del words_in, part_in, out_in
+    left = far_is_left()
+    side_blocks(scale, left, offs, tabs, cnts, halo, perturb, tables, words, part)
+    pack(jnp.where(left, 0, out.shape[1] // 2 // 16 - 1), part, out)
 
 
 VMEM = pl.BlockSpec(memory_space=pltpu.VMEM)
@@ -297,29 +303,29 @@
     )(offs, tabs, cnts, cov, *in_hbm(perturb, control, tables), words, static, edges, mine)
 
 
-def near_blocks(scale, offs, tabs, cnts, halo, perturb, tables, words, part):
+def near_blocks(scale, levels, offs, tabs, cnts, halo, perturb, tables, words, part):
+    lines = part.shape[0] * part.shape[1] // levels
     return pl.pallas_call(
         functools.partial(near_kernel, scale),
-        out_shape=(like(words), like(part)),
+        out_shape=(like(words), like(part), pltpu.VMEM((levels, lines, LANES), jnp.bfloat16)),
         in_specs=[SMEM] * 3 + [VMEM] * 5,
-        out_specs=(VMEM, VMEM),
+        out_specs=(VMEM,) * 3,
         input_output_aliases={6: 0, 7: 1},
         compiler_params=params(16),
         cost_estimate=block_cost(perturb, offs, HB),
     )(offs, tabs, cnts, halo, perturb, tables, words, part)
 
 
-def far_blocks(scale, levels, offs, tabs, cnts, halo, perturb, tables, words, part):
-    lines = part.shape[0] * part.shape[1] // levels
+def far_blocks(scale, offs, tabs, cnts, halo, perturb, tables, words, part, partial):
     return pl.pallas_call(
         functools.partial(far_kernel, scale),
-        out_shape=(pltpu.VMEM((levels, lines, LANES), jnp.bfloat16), like(words), like(part)),
-        in_specs=[SMEM] * 3 + [VMEM] * 5,
-        out_specs=(VMEM, VMEM, VMEM),
-        input_output_aliases={6: 1, 7: 2},
+        out_shape=(like(partial), like(words), like(part)),
+        in_specs=[SMEM] * 3 + [VMEM] * 6,
+        out_specs=(VMEM,) * 3,
+        input_output_aliases={6: 1, 7: 2, 8: 0},
         compiler_params=params(16),
         cost_estimate=block_cost(perturb, offs, HB),
-    )(offs, tabs, cnts, halo, perturb, tables, words, part)[0]
+    )(offs, tabs, cnts, halo, perturb, tables, words, part, partial)[0]
 
 
 def per_device(perturb, control, static_cov, loc_table, pair_offset, pair_table, pair_count):
@@ -343,8 +349,12 @@
     words, static, perturb, tables, part = inner_blocks(
         scale, offs, tabs, cnts, cov, *whole, words, static, edges, tables
     )
-    words, part = near_blocks(scale, offs, tabs, cnts, near, perturb, tables, words, part)
-    partial = far_blocks(scale, levels, offs, tabs, cnts, far, perturb, tables, words, part)
+    words, part, partial = near_blocks(
+        scale, levels, offs, tabs, cnts, near, perturb, tables, words, part
+    )
+    partial = far_blocks(
+        scale, offs, tabs, cnts, far, perturb, tables, words, part, partial
+    )
     owned = lax.all_to_all(partial, "member", split_axis=0, concat_axis=0, tiled=True)
     total = jnp.sum(owned.astype(jnp.float32), axis=0) + static
     return total.reshape(fields, 1, width)

time: 34.7 us -> 34.6 us (level)
  no operation moved by 1% of the time
where the time goes in v6:
time: 34.6 us; the launch traced here: 34.3 us
  blocking collectives  17.3 us (50%)
  Pallas kernels  13.4 us (39%)
  waiting for transfers between devices  1.49 us (4%)
  starting transfers between devices  1.34 us (4%)
  other arithmetic  0.71 us (2%)
    all_to_all x1, blocking collectives, per_device(): lax.all_to_all(partial, 'member', split_axis=0, concat_axis=0, tiled=True)  17.3 us
    pallas_call x1, Pallas kernels, inner_blocks(): pl.pallas_call(functools.partial(inner_kernel, scale), out_shape=(like(wo...  5.54 us
    pallas_call x1, Pallas kernels, load_ahead(): pl.pallas_call(ahead_kernel, out_shape=(like(words), like(static), like(p...  2.38 us
    pallas_call x1, Pallas kernels, near_blocks(): pl.pallas_call(functools.partial(near_kernel, scale), out_shape=(like(wor...  1.93 us
    pallas_call x1, Pallas kernels, far_blocks(): pl.pallas_call(functools.partial(far_kernel, scale), out_shape=(like(part...  1.86 us
    pallas_call x1, Pallas kernels, band_edges(): pl.pallas_call(edge_kernel, out_shape=(send, send, words, pltpu.VMEM((2 *...  1.73 us
    ppermute x1, waiting for transfers between devices, per_device(): far = lax.ppermute(far, 'band', across)  1.48 us
    ppermute x1, starting transfers between devices, per_device(): near = lax.ppermute(near, 'band', beside)  0.76 us
  transfers between devices with their start and end apart: 2, of which 1 were waited for; matrix products, arithmetic and copies ran while one was open for 0% of the time, Pallas kernels for 29%

profile of v6, /device:TPU:97, one launch (start us, length us, event | category | flops | bytes accessed | tf_op | source)
XLA Modules:
  0.0 34.3 jit_solution(11552375533659702505)
XLA Ops:
  0.0 1.7 %shard_map.73 = (bf16[160,1536]{1,0:T(8,128)(2,1)S(1)}, bf16[160,1536]{1,0:T(8,128)(2,1)S(1)}, bf16[160,11520]{1,0:T(8,128)(2,1)S(1)}, f32[128,128]{1,0:T(8,128)...) custom-call(bf16[5,32,8192]{2,1,0:T(8,128)(2,1)} %bitcast.6, ...), custom_call_target="tpu_custom_call" | custom-call | flops 1000000 | bytes 3145728 | tf_op jit(solution)/shard_map/pallas_call | solution.py:252
  1.7 0.8 %collective-permute-start.1 = (bf16[160,1536]{1,0:T(8,128)(2,1)S(1)}, bf16[160,1536]{1,0:T(8,128)(2,1)S(1)}, u32[]{:S(2)}, u32[]{:S(2)}) collective-permute-start(bf16[160,1536]{1,0:T(8,128)(2,1)S(1)} %get-tuple-element.43), channel_id=1, source_target_pairs={{0,1},{1,0},{2,3},{3,2},{4,5},{5,4},{6,7},{7,6},{8,9},{9,8},{10,11... | collective-permute-start | bytes 1474568 | tf_op jit(solution)/shard_map/ppermute | solution.py:345
  2.5 2.4 %shard_map.74 = (bf16[160,11520]{1,0:T(8,128)(2,1)S(1)}, f32[128,128]{1,0:T(8,128)S(1)}, bf16[5,32,8192]{2,1,0:T(8,128)(2,1)S(1)}, bf16[160,1536]{1,0:T(8,128)(2,1)S(1)}, bf16[16,256,256]{2,1,0:T(8,128)(2,1)S(1)}) custom-call(f32[32,16]{1,0:T(8,128)S(4)} %get-tuple-element.31.cov, ...), custom_call_target="tpu_custom_call", output_to_operand_aliasing={{0}: (4, {}), {1}: (5, {}), {2}: (6, {}), {3}: (7, {})} | custom-call | flops 20000000000 | bytes 10000 | tf_op jit(solution)/shard_map/pallas_call | solution.py:277
  4.9 0.6 %collective-permute-start = (bf16[160,1536]{1,0:T(8,128)(2,1)S(1)}, bf16[160,1536]{1,0:T(8,128)(2,1)S(1)}, u32[]{:S(2)}, u32[]{:S(2)}) collective-permute-start(bf16[160,1536]{1,0:T(8,128)(2,1)S(1)} %get-tuple-element.36), channel_id=1, source_target_pairs={{0,15},{1,2},{2,1},{3,4},{4,3},{5,6},{6,5},{7,8},{8,7},{9,10},{10,... | collective-permute-start | bytes 1474568 | tf_op jit(solution)/shard_map/ppermute | solution.py:348
  5.5 5.5 %shard_map.75 = (bf16[160,11520]{1,0:T(8,128)(2,1)S(1)}, f32[128,128]{1,0:T(8,128)S(1)}, bf16[5,32,8192]{2,1,0:T(8,128)(2,1)S(1)}, bf16[16,256,256]{2,1,0:T(8,128)(2,1)S(1)}, f32[64,32,128]{2,1,0:T(8,128)S(1)}) custom-call(s32[12,32]{1,0:T(8,128)S(4)} %get-tuple-element.28.offs, ...), custom_call_target="tpu_custom_call", output_to_operand_aliasing={{0}: (7, {}), {1}: (8, {}), {2}: (9, {}), {3}: (10, {})} | custom-call | flops 100000 | bytes 10000 | tf_op jit(solution)/shard_map/pallas_call | solution.py:291
  11.0 0.0 collective-permute-done.1.halo
  11.0 1.9 %shard_map.76 = (bf16[160,11520]{1,0:T(8,128)(2,1)S(1)}, f32[64,32,128]{2,1,0:T(8,128)S(1)}, bf16[16,128,128]{2,1,0:T(8,128)(2,1)S(1)}) custom-call(s32[12,32]{1,0:T(8,128)S(4)} %get-tuple-element.28.offs, s32[12,32]{1,0:T(8,128)S(4)} %get-tuple-element.29.tabs, s32[32]{0:T(128)S(4)} %get-tuple-element.30.cnts, ...), custom_call_target="tpu_custom_call", output_to_operand_aliasing={{0}: (6, {}), {1}: (7, {})} | custom-call | flops 1509949440 | bytes 3145728 | tf_op jit(solution)/shard_map/pallas_call | solution.py:308
  13.0 1.5 %collective-permute-done.halo = bf16[160,1536]{1,0:T(8,128)(2,1)S(1)} collective-permute-done((bf16[160,1536]{1,0:T(8,128)(2,1)S(1)}, bf16[160,1536]{1,0:T(8,128)(2,1)S(1)}, u32[]{:S(2)}, u32[]{:S(2)}) %collective-permute-start) | collective-permute-done | bytes 491552 | tf_op jit(solution)/shard_map/ppermute | solution.py:348
  14.4 1.9 %shard_map.77 = (bf16[16,128,128]{2,1,0:T(8,128)(2,1)S(1)}, bf16[160,11520]{1,0:T(8,128)(2,1)S(1)}, f32[64,32,128]{2,1,0:T(8,128)S(1)}) custom-call(s32[12,32]{1,0:T(8,128)S(4)} %get-tuple-element.28.offs, s32[12,32]{1,0:T(8,128)S(4)} %get-tuple-element.29.tabs, ...), custom_call_target="tpu_custom_call", output_to_operand_aliasing={{1}: (6, {}), {2}: (7, {}), {0}: (8, {})} | custom-call | flops 1509949440 | bytes 3145728 | tf_op jit(solution)/shard_map/pallas_call | solution.py:320
  16.3 17.3 %all_to_all.5 = bf16[16,128,128]{2,1,0:T(8,128)(2,1)S(1)} all-to-all(bf16[16,128,128]{2,1,0:T(8,128)(2,1)S(1)} %get-tuple-element.49), channel_id=1, replica_groups=mesh['member'=16,'band'=16] {'member'}, dimensions={0} | all-to-all | bytes 1048576 | tf_op jit(solution)/shard_map/all_to_all | solution.py:358
  33.6 0.1 convert_reduce_fusion
  33.7 0.6 %add.3 = f32[128,128]{1,0:T(8,128)} add(f32[128,128]{1,0:T(8,128)S(1)} %convert_reduce_fusion, f32[128,128]{1,0:T(8,128)S(1)} %get-tuple-element.50) | non-fusion elementwise | flops 16384 | bytes 196608 | tf_op jit(solution)/shard_map/add | solution.py:359
Async XLA Ops:
  1.7 9.3 %collective-permute-start.1 = (bf16[160,1536]{1,0:T(8,128)(2,1)S(1)}, bf16[160,1536]{1,0:T(8,128)(2,1)S(1)}, u32[]{:S(2)}, u32[]{:S(2)}) collective-permute-start(bf16[160,1536]{1,0:T(8,128)(2,1)S(1)} %get-tuple-element.43), channel_id=1, source_target_pairs={{0,1},{1,0},{2,3},{3,2},{4,5},{5,4},{6,7},{7,6},{8,9},{9,8},{10,11... | collective-permute-start | bytes 1474568 | tf_op jit(solution)/shard_map/ppermute | solution.py:345
  4.9 9.6 %collective-permute-start = (bf16[160,1536]{1,0:T(8,128)(2,1)S(1)}, bf16[160,1536]{1,0:T(8,128)(2,1)S(1)}, u32[]{:S(2)}, u32[]{:S(2)}) collective-permute-start(bf16[160,1536]{1,0:T(8,128)(2,1)S(1)} %get-tuple-element.36), channel_id=1, source_target_pairs={{0,15},{1,2},{2,1},{3,4},{4,3},{5,6},{6,5},{7,8},{8,7},{9,10},{10,... | collective-permute-start | bytes 1474568 | tf_op jit(solution)/shard_map/ppermute | solution.py:348

commit v7 on v6

--- a/solution.py
+++ b/solution.py
@@ -27,12 +27,13 @@
 
 def block_term(b, zero_block, offs, tabs, cnts, words, tables, perturb, part, scale):
     count = cnts[b]
-    acc = None
-    for s in range(offs.shape[0]):
-        c = jnp.where(s < count, HB + b + offs[s, b], zero_block)
-        lhs = words[:, pl.ds(pl.multiple_of(c * COLS, COLS), COLS)]
-        prod = jnp.dot(lhs, tables[tabs[s, b]], preferred_element_type=jnp.float32)
-        acc = prod if acc is None else acc + prod
+    slots = range(offs.shape[0])
+    cs = [jnp.where(s < count, HB + b + offs[s, b], zero_block) for s in slots]
+    lhs = jnp.concatenate(
+        [words[:, pl.ds(pl.multiple_of(c * COLS, COLS), COLS)] for c in cs], axis=1
+    )
+    rhs = jnp.concatenate([tables[tabs[s, b]] for s in slots], axis=0)
+    acc = jnp.dot(lhs, rhs, preferred_element_type=jnp.float32)
     cols = pl.ds(pl.multiple_of(b * COLS, COLS), COLS)
     members, fl = perturb.shape[0], perturb.shape[1]
     total = None

time: 34.6 us -> 34.5 us (level)
  no operation moved by 1% of the time
where the time goes in v7:
time: 34.5 us; the launch traced here: 34.3 us
  blocking collectives  17.3 us (50%)
  Pallas kernels  13.4 us (39%)
  waiting for transfers between devices  1.49 us (4%)
  starting transfers between devices  1.34 us (4%)
  other arithmetic  0.71 us (2%)
    all_to_all x1, blocking collectives, per_device(): lax.all_to_all(partial, 'member', split_axis=0, concat_axis=0, tiled=True)  17.3 us
    pallas_call x1, Pallas kernels, inner_blocks(): pl.pallas_call(functools.partial(inner_kernel, scale), out_shape=(like(wo...  5.55 us
    pallas_call x1, Pallas kernels, load_ahead(): pl.pallas_call(ahead_kernel, out_shape=(like(words), like(static), like(p...  2.38 us
    pallas_call x1, Pallas kernels, near_blocks(): pl.pallas_call(functools.partial(near_kernel, scale), out_shape=(like(wor...  1.91 us
    pallas_call x1, Pallas kernels, far_blocks(): pl.pallas_call(functools.partial(far_kernel, scale), out_shape=(like(part...  1.85 us
    pallas_call x1, Pallas kernels, band_edges(): pl.pallas_call(edge_kernel, out_shape=(send, send, words, pltpu.VMEM((2 *...  1.73 us
    ppermute x1, waiting for transfers between devices, per_device(): far = lax.ppermute(far, 'band', across)  1.48 us
    ppermute x1, starting transfers between devices, per_device(): near = lax.ppermute(near, 'band', beside)  0.76 us
  transfers between devices with their start and end apart: 2, of which 1 were waited for; matrix products, arithmetic and copies ran while one was open for 0% of the time, Pallas kernels for 29%

profile of v7, /device:TPU:97, one launch (start us, length us, event | category | flops | bytes accessed | tf_op | source)
XLA Modules:
  0.0 34.3 jit_solution(8432427580188451909)
XLA Ops:
  0.0 1.7 %shard_map.73 = (bf16[160,1536]{1,0:T(8,128)(2,1)S(1)}, bf16[160,1536]{1,0:T(8,128)(2,1)S(1)}, bf16[160,11520]{1,0:T(8,128)(2,1)S(1)}, f32[128,128]{1,0:T(8,128)...) custom-call(bf16[5,32,8192]{2,1,0:T(8,128)(2,1)} %bitcast.6, ...), custom_call_target="tpu_custom_call" | custom-call | flops 1000000 | bytes 3145728 | tf_op jit(solution)/shard_map/pallas_call | solution.py:253
  1.7 0.8 %collective-permute-start.1 = (bf16[160,1536]{1,0:T(8,128)(2,1)S(1)}, bf16[160,1536]{1,0:T(8,128)(2,1)S(1)}, u32[]{:S(2)}, u32[]{:S(2)}) collective-permute-start(bf16[160,1536]{1,0:T(8,128)(2,1)S(1)} %get-tuple-element.43), channel_id=1, source_target_pairs={{0,1},{1,0},{2,3},{3,2},{4,5},{5,4},{6,7},{7,6},{8,9},{9,8},{10,11... | collective-permute-start | bytes 1474568 | tf_op jit(solution)/shard_map/ppermute | solution.py:346
  2.5 2.4 %shard_map.74 = (bf16[160,11520]{1,0:T(8,128)(2,1)S(1)}, f32[128,128]{1,0:T(8,128)S(1)}, bf16[5,32,8192]{2,1,0:T(8,128)(2,1)S(1)}, bf16[160,1536]{1,0:T(8,128)(2,1)S(1)}, bf16[16,256,256]{2,1,0:T(8,128)(2,1)S(1)}) custom-call(f32[32,16]{1,0:T(8,128)S(4)} %get-tuple-element.31.cov, ...), custom_call_target="tpu_custom_call", output_to_operand_aliasing={{0}: (4, {}), {1}: (5, {}), {2}: (6, {}), {3}: (7, {})} | custom-call | flops 20000000000 | bytes 10000 | tf_op jit(solution)/shard_map/pallas_call | solution.py:278
  4.9 0.6 %collective-permute-start = (bf16[160,1536]{1,0:T(8,128)(2,1)S(1)}, bf16[160,1536]{1,0:T(8,128)(2,1)S(1)}, u32[]{:S(2)}, u32[]{:S(2)}) collective-permute-start(bf16[160,1536]{1,0:T(8,128)(2,1)S(1)} %get-tuple-element.36), channel_id=1, source_target_pairs={{0,15},{1,2},{2,1},{3,4},{4,3},{5,6},{6,5},{7,8},{8,7},{9,10},{10,... | collective-permute-start | bytes 1474568 | tf_op jit(solution)/shard_map/ppermute | solution.py:349
  5.5 5.5 %shard_map.75 = (bf16[160,11520]{1,0:T(8,128)(2,1)S(1)}, f32[128,128]{1,0:T(8,128)S(1)}, bf16[5,32,8192]{2,1,0:T(8,128)(2,1)S(1)}, bf16[16,256,256]{2,1,0:T(8,128)(2,1)S(1)}, f32[64,32,128]{2,1,0:T(8,128)S(1)}) custom-call(s32[12,32]{1,0:T(8,128)S(4)} %get-tuple-element.28.offs, ...), custom_call_target="tpu_custom_call", output_to_operand_aliasing={{0}: (7, {}), {1}: (8, {}), {2}: (9, {}), {3}: (10, {})} | custom-call | flops 100000 | bytes 10000 | tf_op jit(solution)/shard_map/pallas_call | solution.py:292
  11.0 0.0 collective-permute-done.1.halo
  11.0 1.9 %shard_map.76 = (bf16[160,11520]{1,0:T(8,128)(2,1)S(1)}, f32[64,32,128]{2,1,0:T(8,128)S(1)}, bf16[16,128,128]{2,1,0:T(8,128)(2,1)S(1)}) custom-call(s32[12,32]{1,0:T(8,128)S(4)} %get-tuple-element.28.offs, s32[12,32]{1,0:T(8,128)S(4)} %get-tuple-element.29.tabs, s32[32]{0:T(128)S(4)} %get-tuple-element.30.cnts, ...), custom_call_target="tpu_custom_call", output_to_operand_aliasing={{0}: (6, {}), {1}: (7, {})} | custom-call | flops 1509949440 | bytes 3145728 | tf_op jit(solution)/shard_map/pallas_call | solution.py:309
  13.0 1.5 %collective-permute-done.halo = bf16[160,1536]{1,0:T(8,128)(2,1)S(1)} collective-permute-done((bf16[160,1536]{1,0:T(8,128)(2,1)S(1)}, bf16[160,1536]{1,0:T(8,128)(2,1)S(1)}, u32[]{:S(2)}, u32[]{:S(2)}) %collective-permute-start) | collective-permute-done | bytes 491552 | tf_op jit(solution)/shard_map/ppermute | solution.py:349
  14.4 1.8 %shard_map.77 = (bf16[16,128,128]{2,1,0:T(8,128)(2,1)S(1)}, bf16[160,11520]{1,0:T(8,128)(2,1)S(1)}, f32[64,32,128]{2,1,0:T(8,128)S(1)}) custom-call(s32[12,32]{1,0:T(8,128)S(4)} %get-tuple-element.28.offs, s32[12,32]{1,0:T(8,128)S(4)} %get-tuple-element.29.tabs, ...), custom_call_target="tpu_custom_call", output_to_operand_aliasing={{1}: (6, {}), {2}: (7, {}), {0}: (8, {})} | custom-call | flops 1509949440 | bytes 3145728 | tf_op jit(solution)/shard_map/pallas_call | solution.py:321
  16.3 17.3 %all_to_all.5 = bf16[16,128,128]{2,1,0:T(8,128)(2,1)S(1)} all-to-all(bf16[16,128,128]{2,1,0:T(8,128)(2,1)S(1)} %get-tuple-element.49), channel_id=1, replica_groups=mesh['member'=16,'band'=16] {'member'}, dimensions={0} | all-to-all | bytes 1048576 | tf_op jit(solution)/shard_map/all_to_all | solution.py:359
  33.6 0.1 convert_reduce_fusion
  33.7 0.6 %add.3 = f32[128,128]{1,0:T(8,128)} add(f32[128,128]{1,0:T(8,128)S(1)} %convert_reduce_fusion, f32[128,128]{1,0:T(8,128)S(1)} %get-tuple-element.50) | non-fusion elementwise | flops 16384 | bytes 196608 | tf_op jit(solution)/shard_map/add | solution.py:360
Async XLA Ops:
  1.7 9.3 %collective-permute-start.1 = (bf16[160,1536]{1,0:T(8,128)(2,1)S(1)}, bf16[160,1536]{1,0:T(8,128)(2,1)S(1)}, u32[]{:S(2)}, u32[]{:S(2)}) collective-permute-start(bf16[160,1536]{1,0:T(8,128)(2,1)S(1)} %get-tuple-element.43), channel_id=1, source_target_pairs={{0,1},{1,0},{2,3},{3,2},{4,5},{5,4},{6,7},{7,6},{8,9},{9,8},{10,11... | collective-permute-start | bytes 1474568 | tf_op jit(solution)/shard_map/ppermute | solution.py:346
  4.9 9.6 %collective-permute-start = (bf16[160,1536]{1,0:T(8,128)(2,1)S(1)}, bf16[160,1536]{1,0:T(8,128)(2,1)S(1)}, u32[]{:S(2)}, u32[]{:S(2)}) collective-permute-start(bf16[160,1536]{1,0:T(8,128)(2,1)S(1)} %get-tuple-element.36), channel_id=1, source_target_pairs={{0,15},{1,2},{2,1},{3,4},{4,3},{5,6},{6,5},{7,8},{8,7},{9,10},{10,... | collective-permute-start | bytes 1474568 | tf_op jit(solution)/shard_map/ppermute | solution.py:349
